TPU v7x, 32 devices: a whole 2x2x4 slice. The times are simulated.
32 devices in a mesh: row: 4 (over y, core), col: 8 (over z, x).
Axes of the slice: x: 2, y: 2, z: 4, core: 2. Of those that a mesh axis runs over, the one named last changes fastest.
Arguments:
- b3c_blocks: bfloat16 [16384, 8, 128], P(('row', 'col')), may hold values from -1.5 to 1.5
- pair_index: int32 [128, 8], P(('row', 'col')), may hold values from 0 to 31, all different within a row
- green_occ: bfloat16 [32, 32], replicated, may hold values from -1 to 1
- green_virt: bfloat16 [128, 128], replicated, may hold values from -0.5 to 0.5
Outputs:
- response: float32 [16384, 4, 8, 512], P('row', None, 'col')
Inputs may be any that keep to these rules, and one draw needn't show every extreme that they name: `pair_index`: each row names 8 different values; every value of 0 to 31 is named by some row.
All inputs are finite; a program needn't handle non-finite values.
Results may differ from a plain program's by a relative error of at most 0.0042.
Values may be sent and summed in bfloat16 or wider, within the bound.
No kernel may reach another device: no remote copies, remote signals or barrier semaphores. Data moves between devices by JAX's collectives and lax.ppermute only.
A program may use at most 256 MiB of HBM per device.

v0:
```python
import functools

import jax
import jax.numpy as jnp
import numpy as np
from jax import lax
from jax.experimental import pallas as pl
from jax.experimental.pallas import tpu as pltpu
from jax.sharding import PartitionSpec as P

GROUP = 32
TAIL = 16
SUB = 8
MIB = 1 << 20
VMEM_LIMIT = 24
EARLY, FULL = 24, 18


def names_of(index_ref, first, count, lanes):
    slots = index_ref.shape[1]
    row = lax.broadcasted_iota(jnp.int32, (TAIL, lanes), 0)
    lane = lax.broadcasted_iota(jnp.int32, (TAIL, lanes), 1) % slots
    names = jnp.zeros((TAIL, lanes), jnp.float32)
    for b in range(count):
        for j in range(slots):
            here = (row == b) & (lane == j)
            names = jnp.where(here, index_ref[first + b, j].astype(jnp.float32), names)
    return names.astype(jnp.bfloat16)


def prepare_kernel(index_ref, raw_ref, virt_ref, *out_refs):
    *half_refs, turned_ref = out_refs
    depth = raw_ref.shape[1]
    blocks, slots = index_ref.shape
    rows = turned_ref.shape[1]
    per_piece = blocks // len(half_refs)
    span = raw_ref.shape[0] // len(half_refs)
    for n, half_ref in enumerate(half_refs):
        half = jnp.dot(
            raw_ref[n * span : (n + 1) * span, :], virt_ref[...], preferred_element_type=jnp.float32
        )
        half_ref[:span, :] = half.astype(jnp.bfloat16)
        half_ref[span:, :] = names_of(index_ref, n * per_piece, per_piece, depth)
    span = GROUP * slots
    to = lax.broadcasted_iota(jnp.int32, (span, span), 0)
    at = lax.broadcasted_iota(jnp.int32, (span, span), 1)
    same = (to // GROUP == at % slots) & (to % GROUP == at // slots)
    move = jnp.where(same, 1.0, 0.0).astype(jnp.bfloat16)
    for b in range(blocks):
        base = b * rows * slots
        parts = [
            jnp.dot(
                move,
                raw_ref[base + g * span : base + (g + 1) * span, :],
                preferred_element_type=jnp.float32,
            )
            for g in range(rows // GROUP)
        ]
        for j in range(slots):
            slab = jnp.concatenate([part[j * GROUP : (j + 1) * GROUP, :] for part in parts], axis=0)
            first = (b * slots + j) * depth
            turned_ref[first : first + depth, :] = slab.T.astype(jnp.bfloat16)


def prepare(raw, pair_index, green_virt, pieces, rows):
    span, depth = raw.shape[0] // pieces, raw.shape[1]
    blocks, slots = pair_index.shape
    vmem = pl.BlockSpec(memory_space=pltpu.VMEM)
    *halves, turned = pl.pallas_call(
        prepare_kernel,
        in_specs=[pl.BlockSpec(memory_space=pltpu.SMEM), vmem, vmem],
        out_specs=[vmem] * (pieces + 1),
        out_shape=[jax.ShapeDtypeStruct((span + TAIL, depth), jnp.bfloat16)] * pieces
        + [jax.ShapeDtypeStruct((blocks * slots * depth, rows), jnp.bfloat16)],
        compiler_params=pltpu.CompilerParams(vmem_limit_bytes=62 * MIB),
        name="prepare",
    )(pair_index, raw, green_virt)
    return halves, turned


def mix_pieces(occ_ref, piece_refs, mixed_ref, rows, slots):
    width, _, depth = mixed_ref.shape
    span = piece_refs[0].shape[0] - TAIL
    per_piece = span // (rows * slots)
    wide = GROUP * slots
    level = lax.broadcasted_iota(jnp.int32, (width, wide), 0).astype(jnp.float32)
    to = lax.broadcasted_iota(jnp.int32, (width * GROUP, wide), 0) % GROUP
    same = to == lax.broadcasted_iota(jnp.int32, (width * GROUP, wide), 1) // slots
    named = []
    for piece_ref in piece_refs:
        names = piece_ref[span:, :].astype(jnp.float32)
        for b in range(per_piece):
            name = jnp.concatenate([names[b : b + 1, :]] * (wide // depth), axis=1)
            named.append(jnp.where(level == name, 1.0, 0.0).astype(jnp.bfloat16))
    picked = lax.dot_general(
        occ_ref[...],
        jnp.concatenate(named, axis=1),
        (((0,), (0,)), ((), ())),
        preferred_element_type=jnp.float32,
    )
    for n, piece_ref in enumerate(piece_refs):
        for b in range(per_piece):
            at = (n * per_piece + b) * wide
            mix = jnp.broadcast_to(picked[:, None, at : at + wide], (width, GROUP, wide))
            mix = jnp.where(same, mix.reshape(width * GROUP, wide), 0.0).astype(jnp.bfloat16)
            base = b * rows * slots
            for g in range(0, rows // GROUP, 2):
                right = jnp.concatenate(
                    [
                        piece_ref[base + (g + e) * wide : base + (g + e + 1) * wide, :]
                        for e in range(2)
                    ],
                    axis=1,
                )
                part = jnp.dot(mix, right, preferred_element_type=jnp.float32).astype(jnp.bfloat16)
                for e in range(2):
                    first = (n * per_piece + b) * rows + (g + e) * GROUP
                    mixed_ref[:, first : first + GROUP, :] = part[
                        :, e * depth : (e + 1) * depth
                    ].reshape(width, GROUP, depth)


def panel_kernel(place_ref, occ_ref, *rest, plan):
    (units, kept, owners, extra, keep, token, blocks, slots, first_owner) = plan
    rest = list(rest)
    take = lambda count: [rest.pop(0) for _ in range(count)]
    index_refs = take(owners // 2)
    unit_refs = [take(1 if kept else len(unit)) for unit in units]
    turned_refs = take(owners)
    take(extra)
    out_ref = rest.pop(0)
    for token_ref in take(token):
        token_ref[0] = 0
    mixed_refs = [refs[0] for refs in unit_refs] if kept else take(len(units))
    out_buf, out_sem = rest
    here, depth = mixed_refs[0].shape[1:]
    height = here // len(units[0])
    per_group = SUB // blocks
    stores = []
    here_too = place_ref[0] >= 0
    for u, unit in enumerate(units):
        mixed_ref = mixed_refs[u]
        if not kept:

            @pl.when(here_too)
            def _():
                rows = turned_refs[0].shape[1]
                mix_pieces(occ_ref, unit_refs[u], mixed_ref, rows, slots)

        for g in range(owners // per_group):
            flat = out_buf.at[u, g].reshape(here * SUB, depth)
            tile = place_ref[first_owner + g * per_group] * blocks

            @pl.when(here_too)
            def _():
                for n in range(g * per_group, (g + 1) * per_group):
                    first = lax.rem(place_ref[first_owner + n] * blocks, SUB)
                    for b in range(blocks):
                        left = jnp.concatenate(
                            [
                                mixed_ref[index_refs[n // 2][n % 2 * blocks + b, j]]
                                for j in range(slots)
                            ],
                            axis=1,
                        )
                        right = turned_refs[n][b * slots * depth : (b + 1) * slots * depth, :]
                        flat[pl.ds(first + b, here, stride=SUB), :] = jnp.dot(
                            left, right, preferred_element_type=jnp.float32
                        )

            for n, at in enumerate(unit):
                first = pl.multiple_of(place_ref[at] * height, height)
                store = pltpu.make_async_copy(
                    out_buf.at[u, g, pl.ds(n * height, height)],
                    out_ref.at[pl.ds(first, height), tile // SUB],
                    out_sem.at[u, g, n],
                )
                store.start()
                stores.append(store)
    for store in stores:
        store.wait()


def make_panel(
    place, green_occ, index, units, at, turned, first_owner, sizes, before, keep, kept, token
):
    blocks, slots, width, total, groups, height = sizes
    depth, rows = turned[0].shape[0] // (blocks * slots), turned[0].shape[1]
    owners = len(turned)
    here = len(at[0]) * height
    own_groups = owners * blocks // SUB
    extra = [] if before is None else [before]
    flat = [a for unit in units for a in unit]
    plan = (at, kept, owners, len(extra), keep, token, blocks, slots, first_owner)
    anywhere = pl.BlockSpec(memory_space=pl.ANY)
    smem = pl.BlockSpec(memory_space=pltpu.SMEM)
    vmem = pl.BlockSpec(memory_space=pltpu.VMEM)
    mixed = jax.ShapeDtypeStruct((width, here, depth), jnp.bfloat16)
    out = jax.ShapeDtypeStruct((total, groups, SUB, depth), jnp.float32)
    count = len(units)
    return pl.pallas_call(
        functools.partial(panel_kernel, plan=plan),
        in_specs=[smem, vmem]
        + [smem] * len(index)
        + [vmem] * (len(flat) + owners)
        + [anywhere] * len(extra),
        out_specs=[anywhere] + [smem] * token + [vmem] * (count * keep),
        out_shape=[out]
        + [jax.ShapeDtypeStruct((1,), jnp.int32)] * token
        + [mixed] * (count * keep),
        scratch_shapes=[pltpu.VMEM(mixed.shape, mixed.dtype)] * (0 if keep or kept else count)
        + [
            pltpu.VMEM((count, own_groups, here, SUB, depth), jnp.float32),
            pltpu.SemaphoreType.DMA((count, own_groups, len(at[0]))),
        ],
        input_output_aliases={2 + len(index) + len(flat) + owners: 0} if extra else {},
        compiler_params=pltpu.CompilerParams(vmem_limit_bytes=VMEM_LIMIT * MIB),
        cost_estimate=pl.CostEstimate(
            flops=(EARLY if keep else FULL) * count * here * owners * blocks * rows * slots * depth,
            bytes_accessed=4 * count * here * owners * blocks * rows,
            transcendentals=0,
        ),
        name="panel",
    )(place, green_occ, *index, *flat, *turned, *extra)


def after_kernel(token_ref, array_ref, out_ref):
    out_ref[...] = array_ref[...]


def after(token, array):
    vmem = pl.BlockSpec(memory_space=pltpu.VMEM)
    return pl.pallas_call(
        after_kernel,
        in_specs=[pl.BlockSpec(memory_space=pl.ANY), vmem],
        out_specs=vmem,
        out_shape=jax.ShapeDtypeStruct(array.shape, array.dtype),
        compiler_params=pltpu.CompilerParams(vmem_limit_bytes=4 * MIB),
        name="after",
    )(token, array)


def cycle(count):
    return list(range(0, count, 2)) + list(range(1, count, 2))[::-1]


def ring(count):
    walk = cycle(count)
    return [
        (2 * walk[n] + e, 2 * walk[(n + 1) % count] + e) for n in range(count) for e in range(2)
    ]


def swap(count):
    return [(n, n ^ 1) for n in range(count)]


def behind(index, steps, count):
    walk = cycle(count)
    return 2 * walk[(walk.index(index // 2) - steps) % count] + index % 2


def on_device(b3c_blocks, pair_index, green_occ, green_virt):
    per_device, slots, depth = b3c_blocks.shape
    blocks = pair_index.shape[0]
    rows = per_device // blocks
    n_row, n_col = lax.axis_size("row"), lax.axis_size("col")
    row, col = lax.axis_index("row"), lax.axis_index("col")
    outer, outer_row = n_col // 2, n_row // 2
    cuts = 2 if blocks % 2 == 0 else 1
    total = n_col * per_device
    groups = n_row * blocks // SUB
    split = 2 * blocks == SUB
    sizes = (blocks, slots, green_occ.shape[0], total, groups, per_device // cuts)
    raw = b3c_blocks.reshape(per_device * slots, depth)

    turn_col = functools.partial(lax.ppermute, axis_name="col", perm=ring(outer))
    swap_col = functools.partial(lax.ppermute, axis_name="col", perm=swap(n_col))
    turn_row = functools.partial(lax.ppermute, axis_name="row", perm=ring(outer_row))
    swap_row = functools.partial(lax.ppermute, axis_name="row", perm=swap(n_row))

    every = [(k, e, n) for k in range(outer) for e in range(2) for n in range(cuts)]
    number = {key: n_row + n for n, key in enumerate(every)}
    table = np.zeros((n_row, n_col, n_row + len(every)), np.int32)
    for r in range(n_row):
        for n in range(n_row):
            table[r, :, n] = behind(r, n // 2, outer_row) ^ (n % 2)
    for c in range(n_col):
        for key in every:
            k, e, cut = key
            table[:, c, number[key]] = (behind(c, k, outer) ^ e) * cuts + cut
    place = lax.dynamic_index_in_dim(
        jnp.asarray(table).reshape(n_row * n_col, -1), row * n_col + col, 0, keepdims=False
    )

    held, kept, state = {}, {}, {"panel": None}
    halves, turned = prepare(raw, pair_index, green_virt, cuts, rows)
    for n, piece in enumerate(halves):
        held[0, 0, n] = piece
    turned = [turned]
    for k in range(outer_row - 1):
        turned.append(turn_row(turned[-1]))
    paired = outer == 4 and cuts == 2 and split and outer_row == 2
    if not paired:
        turned = [a for t in turned for a in (t, swap_row(t))]
    index = [jnp.concatenate([pair_index, swap_row(pair_index)], axis=0)]
    for k in range(outer_row - 1):
        index.append(turn_row(index[-1]))

    def step(k, n):
        held[k, 0, n] = turn_col(held[k - 1, 0, n])

    def cross(k, n):
        held[k, 1, n] = swap_col(held[k, 0, n])

    def panel(units, first, count, keep=False, reuse=False, token=False):
        at = [[number[key] for key in unit] for unit in units]
        data = [[kept[tuple(unit)]] if reuse else [held[key] for key in unit] for unit in units]
        here = index[first // 2 : (first + count) // 2]
        state["panel"], *more = make_panel(
            place, green_occ, here, data, at, turned[first : first + count], first, sizes,
            state["panel"], keep, reuse, token,
        )
        if token:
            return more[0]
        for unit, array in zip(units, more):
            kept[tuple(unit)] = array

    if paired:
        A, B = 0, 1
        turned = [turned[0], swap_row(turned[0]), turned[1]]
        for n in range(2):
            step(1, n)
            cross(0, n)
            step(2, n)
        cross(1, A)
        early = [
            [(0, 0, A), (0, 0, B)], [(1, 0, A), (0, 1, A)], [(1, 0, B), (0, 1, B)]
        ]
        for unit in early[:2]:
            panel([unit], 0, 2, keep=True)
        turned.append(swap_row(turned[2]))
        panel(early[2:], 0, 2, keep=True)
        held[2, 0, A] = after(kept[tuple(early[2])], held[2, 0, A])
        step(3, A)
        cross(2, A)
        token = panel(early, 2, 2, reuse=True, token=True)
        held[2, 0, B] = after(token, held[2, 0, B])
        step(3, B)
        cross(2, B)
        token = panel([[(2, 0, A), (1, 1, A)]], 0, 4, token=True)
        held[3, 0, A] = after(token, held[3, 0, A])
        cross(3, A)
        held[1, 1, B] = turn_col(after(token, held[0, 1, B]))
        token = panel([[(2, 0, B), (2, 1, A)]], 0, 4, token=True)
        held[3, 0, B] = after(token, held[3, 0, B])
        cross(3, B)
        panel([[(3, 0, A), (2, 1, B)], [(3, 0, B), (3, 1, A)]], 0, 4)
        panel([[(1, 1, B), (3, 1, B)]], 0, 4)
    else:
        for k in range(outer):
            for n in range(cuts):
                if k > 0:
                    step(k, n)
                cross(k, n)
        for key in every:
            panel([[key]], 0, n_row)
    return state["panel"].reshape(total, n_row, 1, per_device)


def solution(mesh):
    return jax.shard_map(
        on_device,
        mesh=mesh,
        in_specs=(P(("row", "col"), None, None), P(("row", "col"), None), P(), P()),
        out_specs=P("row", None, "col", None),
        check_vma=False,
    )
```

profile of v0, /device:TPU:0, one launch (start us, length us, event | category | flops | bytes accessed | tf_op | source)
XLA Modules:
  0.0 105.9 jit_solution(11338468545371632424)
XLA Ops:
  0.0 0.0 copy-start.3
  0.0 3.6 %prepare.1 = (bf16[2064,128]{1,0:T(8,128)(2,1)}, bf16[2064,128]{1,0:T(8,128)(2,1)}, bf16[4096,128]{1,0:T(8,128)(2,1)}) custom-call(s32[4,8]{1,0:T(4,128)} %index_ref.1, bf16[4096,128]{1,0:T(8,128)(2,1)} %bitcast.4, bf16[128,128]{1,0:T(8,128)(2,1)} %virt_ref.1), custom_call_target="tpu_custom_call" | custom-call | tf_op jit(solution)/shard_map/prepare/pallas_call | solution.py:69
  3.6 0.4 collective-permute-start.4
  4.0 0.1 collective-permute-start
  4.1 4.0 %collective-permute-start.5 = (bf16[2064,128]{1,0:T(8,128)(2,1)}, bf16[2064,128]{1,0:T(8,128)(2,1)S(1)}, u32[]{:S(2)}, u32[]{:S(2)}) collective-permute-start(bf16[2064,128]{1,0:T(8,128)(2,1)} %get-tuple-element.22.rest_1_), channel_id=1, source_target_pairs={{0,4},{1,5},{4,6},{5,7},{6,2},{7,3},{2,0},{3,1},{8,12},{9,13},{12,... | collective-permute-start | bytes 1585160 | tf_op jit(solution)/shard_map/ppermute | solution.py:311
  8.1 1.5 %collective-permute-start.6 = (bf16[2064,128]{1,0:T(8,128)(2,1)}, bf16[2064,128]{1,0:T(8,128)(2,1)S(1)}, u32[]{:S(2)}, u32[]{:S(2)}) collective-permute-start(bf16[2064,128]{1,0:T(8,128)(2,1)} %get-tuple-element.22.rest_1_), channel_id=1, source_target_pairs={{0,1},{1,0},{2,3},{3,2},{4,5},{5,4},{6,7},{7,6},{8,9},{9,8},{10,11... | collective-permute-start | bytes 1585160 | tf_op jit(solution)/shard_map/ppermute | solution.py:314
  9.6 1.6 %collective-permute-start.2 = (bf16[2064,128]{1,0:T(8,128)(2,1)}, bf16[2064,128]{1,0:T(8,128)(2,1)S(1)}, u32[]{:S(2)}, u32[]{:S(2)}) collective-permute-start(bf16[2064,128]{1,0:T(8,128)(2,1)} %get-tuple-element.20.rest_2_), channel_id=1, source_target_pairs={{0,4},{1,5},{4,6},{5,7},{6,2},{7,3},{2,0},{3,1},{8,12},{9,13},{12,... | collective-permute-start | bytes 1585160 | tf_op jit(solution)/shard_map/ppermute | solution.py:311
  11.2 0.7 dynamic-slice_bitcast_fusion.place_ref
  11.9 0.0 collective-permute-done
  11.9 0.5 collective-permute-start.3
  12.4 0.7 pad_add_fusion.rest_0_
  13.1 0.0 collective-permute-done.4.rest_4_.rest_5_.rest_7_
  13.1 1.6 %collective-permute-start.9 = (bf16[4096,128]{1,0:T(8,128)(2,1)}, bf16[4096,128]{1,0:T(8,128)(2,1)S(1)}, u32[]{:S(2)}, u32[]{:S(2)}) collective-permute-start(bf16[4096,128]{1,0:T(8,128)(2,1)} %get-tuple-element.21.rest_3_.rest_4_.rest_6_), channel_id=1, source_target_pairs={{0,16},{8,24},{16,0},{24,8},{1,17},{9,25},{17,1},{25,9},{2,18},{10... | collective-permute-start | bytes 3145736 | tf_op jit(solution)/shard_map/ppermute | solution.py:302
  14.7 0.0 copy-start
  14.7 1.3 %copy-done = bf16[4096,128]{1,0:T(8,128)(2,1)S(1)} copy-done((bf16[4096,128]{1,0:T(8,128)(2,1)S(1)}, bf16[4096,128]{1,0:T(8,128)(2,1)}, u32[]{:S(2)}) %copy-start) | copy-done | bytes 1048600
  15.9 0.0 copy-start.2
  15.9 0.7 copy-done.2
  16.6 0.0 copy-start.4
  16.6 1.0 copy-done.4
  17.7 1.0 copy-done.5
  18.7 0.0 copy-start.1
  18.7 5.7 %panel.8 = (f32[4096,2,8,128]{3,2,1,0:T(8,128)}, bf16[32,512,128]{2,1,0:T(8,128)(2,1)S(1)}) custom-call(s32[20]{0:T(128)S(1)} %dynamic-slice_bitcast_fusion.place_ref, bf16[32,32]{1,0:T(8,128)(2,1)S(1)} %copy-done.2, s32[8,8]{1,0:T(8,128)S(1)} %pad_add_fusion.rest_0_, bf16[2064,128]{1,0:T(8,128)(2,1)S(1)} %copy-done.5, bf16[2064,128]{1,0:T(8,128)(2,1)S(1)} %copy-done.4, ...), custom_call_target="tpu_custom_call" | custom-call | flops 12884901888 | bytes 2097152 | tf_op jit(solution)/shard_map/panel/pallas_call | solution.py:201
  24.4 0.0 collective-permute-done.5.rest_1_
  24.5 0.6 collective-permute-start.1
  25.0 0.0 collective-permute-done.6.rest_2_
  25.0 0.6 collective-permute-start.7
  25.6 0.0 copy-done.3
  25.6 0.0 copy-done.1
  25.6 5.7 %panel.9 = (f32[4096,2,8,128]{3,2,1,0:T(8,128)}, bf16[32,512,128]{2,1,0:T(8,128)(2,1)S(1)}) custom-call(s32[20]{0:T(128)S(1)} %dynamic-slice_bitcast_fusion.place_ref, bf16[32,32]{1,0:T(8,128)(2,1)S(1)} %copy-done.3, s32[8,8]{1,0:T(8,128)S(1)} %pad_add_fusion.rest_0_, ...), custom_call_target="tpu_custom_call", output_to_operand_aliasing={{0}: (7, {})} | custom-call | flops 12884901888 | bytes 2097152 | tf_op jit(solution)/shard_map/panel/pallas_call | solution.py:201
  31.3 0.8 collective-permute-done.2.rest_1_
  32.1 1.5 %collective-permute-start.8 = (bf16[2064,128]{1,0:T(8,128)(2,1)S(1)}, bf16[2064,128]{1,0:T(8,128)(2,1)S(1)}, u32[]{:S(2)}, u32[]{:S(2)}) collective-permute-start(bf16[2064,128]{1,0:T(8,128)(2,1)S(1)} %collective-permute-done.5.rest_1_), channel_id=1, source_target_pairs={{0,1},{1,0},{2,3},{3,2},{4,5},{5,4},{6,7},{7,6},{8,9},{9,8},{10,11... | collective-permute-start | bytes 1585160 | tf_op jit(solution)/shard_map/ppermute | solution.py:314
  33.6 0.0 collective-permute-done.3.rest_2_.array_ref
  33.6 3.3 %collective-permute-start.12 = (bf16[2064,128]{1,0:T(8,128)(2,1)S(1)}, bf16[2064,128]{1,0:T(8,128)(2,1)S(1)}, u32[]{:S(2)}, u32[]{:S(2)}) collective-permute-start(bf16[2064,128]{1,0:T(8,128)(2,1)S(1)} %collective-permute-done.2.rest_1_), channel_id=1, source_target_pairs={{0,4},{1,5},{4,6},{5,7},{6,2},{7,3},{2,0},{3,1},{8,12},{9,13},{12,... | collective-permute-start | bytes 1585160 | tf_op jit(solution)/shard_map/ppermute | solution.py:311
  36.9 0.4 collective-permute-done.9.rest_4_.rest_6_.rest_8_
  37.4 0.0 collective-permute-start.10
  37.4 5.7 %panel.10 = (f32[4096,2,8,128]{3,2,1,0:T(8,128)}, bf16[32,512,128]{2,1,0:T(8,128)(2,1)S(1)}) custom-call(s32[20]{0:T(128)S(1)} %dynamic-slice_bitcast_fusion.place_ref, bf16[32,32]{1,0:T(8,128)(2,1)S(1)} %copy-done.3, s32[8,8]{1,0:T(8,128)S(1)} %pad_add_fusion.rest_0_, ...), custom_call_target="tpu_custom_call", output_to_operand_aliasing={{0}: (7, {})} | custom-call | flops 12884901888 | bytes 2097152 | tf_op jit(solution)/shard_map/panel/pallas_call | solution.py:201
  43.1 0.3 collective-permute-done.7.array_ref
  43.4 3.4 %collective-permute-start.16 = (bf16[2064,128]{1,0:T(8,128)(2,1)S(1)}, bf16[2064,128]{1,0:T(8,128)(2,1)S(1)}, u32[]{:S(2)}, u32[]{:S(2)}) collective-permute-start(bf16[2064,128]{1,0:T(8,128)(2,1)S(1)} %after.5.rest_2_), channel_id=1, source_target_pairs={{0,4},{1,5},{4,6},{5,7},{6,2},{7,3},{2,0},{3,1},{8,12},{9,13},{12,... | collective-permute-start | bytes 1585160 | tf_op jit(solution)/shard_map/ppermute | solution.py:311
  46.8 0.0 collective-permute-done.1.rest_0_.rest_1_
  46.8 1.5 %collective-permute-start.13 = (bf16[2064,128]{1,0:T(8,128)(2,1)S(1)}, bf16[2064,128]{1,0:T(8,128)(2,1)S(1)}, u32[]{:S(2)}, u32[]{:S(2)}) collective-permute-start(bf16[2064,128]{1,0:T(8,128)(2,1)S(1)} %after.5.rest_2_), channel_id=1, source_target_pairs={{0,1},{1,0},{2,3},{3,2},{4,5},{5,4},{6,7},{7,6},{8,9},{9,8},{10,11... | collective-permute-start | bytes 1585160 | tf_op jit(solution)/shard_map/ppermute | solution.py:314
  48.3 0.0 collective-permute-done.10.rest_5_.rest_7_.rest_9_
  48.3 9.7 %panel.11 = (f32[4096,2,8,128]{3,2,1,0:T(8,128)}, s32[1]{0:T(128)}) custom-call(s32[20]{0:T(128)S(1)} %dynamic-slice_bitcast_fusion.place_ref, bf16[32,32]{1,0:T(8,128)(2,1)S(1)} %copy-done.3, s32[8,8]{1,0:T(8,128)S(1)} %collective-permute-done.1.rest_0_.rest_1_, ...), custom_call_target="tpu_custom_call", output_to_operand_aliasing={{0}: (8, {})} | custom-call | flops 28991029248 | bytes 6291456 | tf_op jit(solution)/shard_map/panel/pallas_call | solution.py:201
  58.0 0.0 collective-permute-done.12.array_ref
  58.1 0.7 after.7.rest_2_
  58.8 0.7 collective-permute-start.14
  59.5 0.8 collective-permute-start.17
  60.3 0.0 collective-permute-done.8.rest_3_
  60.3 8.6 %panel.12 = (f32[4096,2,8,128]{3,2,1,0:T(8,128)}, s32[1]{0:T(128)}) custom-call(s32[20]{0:T(128)S(1)} %dynamic-slice_bitcast_fusion.place_ref, bf16[32,32]{1,0:T(8,128)(2,1)S(1)} %copy-done.3, s32[8,8]{1,0:T(8,128)S(1)} %pad_add_fusion.rest_0_, s32[8,8]{1,0:T(8,128)S(1)} %collective-permute-done.1.rest_0_.rest_1_, ...), custom_call_target="tpu_custom_call", output_to_operand_aliasing={{0}: (10, {})} | custom-call | flops 19327352832 | bytes 4194304 | tf_op jit(solution)/shard_map/panel/pallas_call | solution.py:201
  69.0 0.0 collective-permute-done.16.array_ref
  69.0 0.7 after.9.rest_2_
  69.7 1.3 %collective-permute-start.18 = (bf16[2064,128]{1,0:T(8,128)(2,1)S(1)}, bf16[2064,128]{1,0:T(8,128)(2,1)S(1)}, u32[]{:S(2)}, u32[]{:S(2)}) collective-permute-start(bf16[2064,128]{1,0:T(8,128)(2,1)S(1)} %after.9.rest_2_), channel_id=1, source_target_pairs={{0,1},{1,0},{2,3},{3,2},{4,5},{5,4},{6,7},{7,6},{8,9},{9,8},{10,11... | collective-permute-start | bytes 1585160 | tf_op jit(solution)/shard_map/ppermute | solution.py:314
  71.0 0.7 after.6
  71.7 1.3 %collective-permute-start.11 = (bf16[2064,128]{1,0:T(8,128)(2,1)S(1)}, bf16[2064,128]{1,0:T(8,128)(2,1)S(1)}, u32[]{:S(2)}, u32[]{:S(2)}) collective-permute-start(bf16[2064,128]{1,0:T(8,128)(2,1)S(1)} %after.6), channel_id=1, source_target_pairs={{0,4},{1,5},{4,6},{5,7},{6,2},{7,3},{2,0},{3,1},{8,12},{9,13},{12,... | collective-permute-start | bytes 1585160 | tf_op jit(solution)/shard_map/ppermute | solution.py:354
  73.0 0.0 collective-permute-done.13.rest_3_
  73.0 8.6 %panel.13 = (f32[4096,2,8,128]{3,2,1,0:T(8,128)}, s32[1]{0:T(128)}) custom-call(s32[20]{0:T(128)S(1)} %dynamic-slice_bitcast_fusion.place_ref, bf16[32,32]{1,0:T(8,128)(2,1)S(1)} %copy-done.3, s32[8,8]{1,0:T(8,128)S(1)} %pad_add_fusion.rest_0_, s32[8,8]{1,0:T(8,128)S(1)} %collective-permute-done.1.rest_0_.rest_1_, ...), custom_call_target="tpu_custom_call", output_to_operand_aliasing={{0}: (10, {})} | custom-call | flops 19327352832 | bytes 4194304 | tf_op jit(solution)/shard_map/panel/pallas_call | solution.py:201
  81.7 0.0 collective-permute-done.14.array_ref
  81.7 0.7 after.8.rest_4_
  82.4 0.6 collective-permute-start.15
  83.0 0.0 collective-permute-done.18.rest_5_
  83.0 0.0 collective-permute-done.17.rest_3_
  83.0 14.5 %panel.14.rest_8_ = f32[4096,2,8,128]{3,2,1,0:T(8,128)} custom-call(s32[20]{0:T(128)S(1)} %dynamic-slice_bitcast_fusion.place_ref, bf16[32,32]{1,0:T(8,128)(2,1)S(1)} %copy-done.3, s32[8,8]{1,0:T(8,128)S(1)} %pad_add_fusion.rest_0_, s32[8,8]{1,0:T(8,128)S(1)} %collective-permute-done.1.rest_0_.rest_1_, ...), custom_call_target="tpu_custom_call", output_to_operand_aliasing={{}: (12, {})} | custom-call | flops 38654705664 | bytes 8388608 | tf_op jit(solution)/shard_map/panel/pallas_call | solution.py:201
  97.5 0.0 collective-permute-done.11.rest_2_
  97.5 0.0 collective-permute-done.15.rest_3_
  97.5 8.1 %panel.15 = f32[4096,2,8,128]{3,2,1,0:T(8,128)} custom-call(s32[20]{0:T(128)S(1)} %dynamic-slice_bitcast_fusion.place_ref, bf16[32,32]{1,0:T(8,128)(2,1)S(1)} %copy-done.3, s32[8,8]{1,0:T(8,128)S(1)} %pad_add_fusion.rest_0_, s32[8,8]{1,0:T(8,128)S(1)} %collective-permute-done.1.rest_0_.rest_1_, ...), custom_call_target="tpu_custom_call", output_to_operand_aliasing={{}: (10, {})} | custom-call | flops 19327352832 | bytes 4194304 | tf_op jit(solution)/shard_map/panel/pallas_call | solution.py:201
  (2 shorter events, 0.0 us)
Async XLA Ops:
  0.0 25.6 %copy-start.3 = (bf16[32,32]{1,0:T(8,128)(2,1)S(1)}, bf16[32,32]{1,0:T(8,128)(2,1)}, u32[]{:S(2)}) copy-start(bf16[32,32]{1,0:T(8,128)(2,1)} %occ_ref.15) | copy-start | bytes 6148
  3.6 9.5 %collective-permute-start.4 = (bf16[4096,128]{1,0:T(8,128)(2,1)}, bf16[4096,128]{1,0:T(8,128)(2,1)S(1)}, u32[]{:S(2)}, u32[]{:S(2)}) collective-permute-start(bf16[4096,128]{1,0:T(8,128)(2,1)} %get-tuple-element.21.rest_3_.rest_4_.rest_6_), channel_id=1, source_target_pairs={{0,8},{8,0},{16,24},{24,16},{1,9},{9,1},{17,25},{25,17},{2,10},{10... | collective-permute-start | bytes 3145736 | tf_op jit(solution)/shard_map/ppermute | solution.py:331
  4.0 7.9 %collective-permute-start = (s32[4,8]{1,0:T(4,128)}, s32[4,8]{1,0:T(4,128)S(1)}, u32[]{:S(2)}, u32[]{:S(2)}) collective-permute-start(s32[4,8]{1,0:T(4,128)} %index_ref.1), channel_id=1, source_target_pairs={{0,8},{8,0},{16,24},{24,16},{1,9},{9,1},{17,25},{25,17},{2,10},{10... | collective-permute-start | bytes 392 | tf_op jit(solution)/shard_map/ppermute | solution.py:306
  4.1 20.4 %collective-permute-start.5 = (bf16[2064,128]{1,0:T(8,128)(2,1)}, bf16[2064,128]{1,0:T(8,128)(2,1)S(1)}, u32[]{:S(2)}, u32[]{:S(2)}) collective-permute-start(bf16[2064,128]{1,0:T(8,128)(2,1)} %get-tuple-element.22.rest_1_), channel_id=1, source_target_pairs={{0,4},{1,5},{4,6},{5,7},{6,2},{7,3},{2,0},{3,1},{8,12},{9,13},{12,... | collective-permute-start | bytes 1585160 | tf_op jit(solution)/shard_map/ppermute | solution.py:311
  8.1 16.9 %collective-permute-start.6 = (bf16[2064,128]{1,0:T(8,128)(2,1)}, bf16[2064,128]{1,0:T(8,128)(2,1)S(1)}, u32[]{:S(2)}, u32[]{:S(2)}) collective-permute-start(bf16[2064,128]{1,0:T(8,128)(2,1)} %get-tuple-element.22.rest_1_), channel_id=1, source_target_pairs={{0,1},{1,0},{2,3},{3,2},{4,5},{5,4},{6,7},{7,6},{8,9},{9,8},{10,11... | collective-permute-start | bytes 1585160 | tf_op jit(solution)/shard_map/ppermute | solution.py:314
  9.6 22.5 %collective-permute-start.2 = (bf16[2064,128]{1,0:T(8,128)(2,1)}, bf16[2064,128]{1,0:T(8,128)(2,1)S(1)}, u32[]{:S(2)}, u32[]{:S(2)}) collective-permute-start(bf16[2064,128]{1,0:T(8,128)(2,1)} %get-tuple-element.20.rest_2_), channel_id=1, source_target_pairs={{0,4},{1,5},{4,6},{5,7},{6,2},{7,3},{2,0},{3,1},{8,12},{9,13},{12,... | collective-permute-start | bytes 1585160 | tf_op jit(solution)/shard_map/ppermute | solution.py:311
  11.9 21.8 %collective-permute-start.3 = (bf16[2064,128]{1,0:T(8,128)(2,1)}, bf16[2064,128]{1,0:T(8,128)(2,1)S(1)}, u32[]{:S(2)}, u32[]{:S(2)}) collective-permute-start(bf16[2064,128]{1,0:T(8,128)(2,1)} %get-tuple-element.20.rest_2_), channel_id=1, source_target_pairs={{0,1},{1,0},{2,3},{3,2},{4,5},{5,4},{6,7},{7,6},{8,9},{9,8},{10,11... | collective-permute-start | bytes 1585160 | tf_op jit(solution)/shard_map/ppermute | solution.py:314
  13.1 24.3 %collective-permute-start.9 = (bf16[4096,128]{1,0:T(8,128)(2,1)}, bf16[4096,128]{1,0:T(8,128)(2,1)S(1)}, u32[]{:S(2)}, u32[]{:S(2)}) collective-permute-start(bf16[4096,128]{1,0:T(8,128)(2,1)} %get-tuple-element.21.rest_3_.rest_4_.rest_6_), channel_id=1, source_target_pairs={{0,16},{8,24},{16,0},{24,8},{1,17},{9,25},{17,1},{25,9},{2,18},{10... | collective-permute-start | bytes 3145736 | tf_op jit(solution)/shard_map/ppermute | solution.py:302
  14.7 1.3 %copy-start = (bf16[4096,128]{1,0:T(8,128)(2,1)S(1)}, bf16[4096,128]{1,0:T(8,128)(2,1)}, u32[]{:S(2)}) copy-start(bf16[4096,128]{1,0:T(8,128)(2,1)} %get-tuple-element.21.rest_3_.rest_4_.rest_6_) | copy-start | bytes 3145732
  15.9 0.7 copy-start.2
  16.6 1.0 copy-start.4
  17.7 1.0 copy-start.5
  18.7 6.9 %copy-start.1 = (bf16[4096,128]{1,0:T(8,128)(2,1)S(1)}, bf16[4096,128]{1,0:T(8,128)(2,1)}, u32[]{:S(2)}) copy-start(bf16[4096,128]{1,0:T(8,128)(2,1)} %get-tuple-element.21.rest_3_.rest_4_.rest_6_) | copy-start | bytes 3145732
  24.5 22.4 %collective-permute-start.1 = (s32[8,8]{1,0:T(8,128)S(1)}, s32[8,8]{1,0:T(8,128)S(1)}, u32[]{:S(2)}, u32[]{:S(2)}) collective-permute-start(s32[8,8]{1,0:T(8,128)S(1)} %pad_add_fusion.rest_0_), channel_id=1, source_target_pairs={{0,16},{8,24},{16,0},{24,8},{1,17},{9,25},{17,1},{25,9},{2,18},{10... | collective-permute-start | bytes 776 | tf_op jit(solution)/shard_map/ppermute | solution.py:308
  25.0 18.3 %collective-permute-start.7 = (bf16[2064,128]{1,0:T(8,128)(2,1)S(1)}, bf16[2064,128]{1,0:T(8,128)(2,1)S(1)}, u32[]{:S(2)}, u32[]{:S(2)}) collective-permute-start(bf16[2064,128]{1,0:T(8,128)(2,1)S(1)} %collective-permute-done.5.rest_1_), channel_id=1, source_target_pairs={{0,4},{1,5},{4,6},{5,7},{6,2},{7,3},{2,0},{3,1},{8,12},{9,13},{12,... | collective-permute-start | bytes 1585160 | tf_op jit(solution)/shard_map/ppermute | solution.py:311
  32.1 28.2 %collective-permute-start.8 = (bf16[2064,128]{1,0:T(8,128)(2,1)S(1)}, bf16[2064,128]{1,0:T(8,128)(2,1)S(1)}, u32[]{:S(2)}, u32[]{:S(2)}) collective-permute-start(bf16[2064,128]{1,0:T(8,128)(2,1)S(1)} %collective-permute-done.5.rest_1_), channel_id=1, source_target_pairs={{0,1},{1,0},{2,3},{3,2},{4,5},{5,4},{6,7},{7,6},{8,9},{9,8},{10,11... | collective-permute-start | bytes 1585160 | tf_op jit(solution)/shard_map/ppermute | solution.py:314
  33.6 24.4 %collective-permute-start.12 = (bf16[2064,128]{1,0:T(8,128)(2,1)S(1)}, bf16[2064,128]{1,0:T(8,128)(2,1)S(1)}, u32[]{:S(2)}, u32[]{:S(2)}) collective-permute-start(bf16[2064,128]{1,0:T(8,128)(2,1)S(1)} %collective-permute-done.2.rest_1_), channel_id=1, source_target_pairs={{0,4},{1,5},{4,6},{5,7},{6,2},{7,3},{2,0},{3,1},{8,12},{9,13},{12,... | collective-permute-start | bytes 1585160 | tf_op jit(solution)/shard_map/ppermute | solution.py:311
  37.4 11.0 %collective-permute-start.10 = (bf16[4096,128]{1,0:T(8,128)(2,1)S(1)}, bf16[4096,128]{1,0:T(8,128)(2,1)S(1)}, u32[]{:S(2)}, u32[]{:S(2)}) collective-permute-start(bf16[4096,128]{1,0:T(8,128)(2,1)S(1)} %collective-permute-done.9.rest_4_.rest_6_.rest_8_), channel_id=1, source_target_pairs={{0,8},{8,0},{16,24},{24,16},{1,9},{9,1},{17,25},{25,17},{2,10},{10... | collective-permute-start | bytes 3145736 | tf_op jit(solution)/shard_map/ppermute | solution.py:342
  43.4 25.6 %collective-permute-start.16 = (bf16[2064,128]{1,0:T(8,128)(2,1)S(1)}, bf16[2064,128]{1,0:T(8,128)(2,1)S(1)}, u32[]{:S(2)}, u32[]{:S(2)}) collective-permute-start(bf16[2064,128]{1,0:T(8,128)(2,1)S(1)} %after.5.rest_2_), channel_id=1, source_target_pairs={{0,4},{1,5},{4,6},{5,7},{6,2},{7,3},{2,0},{3,1},{8,12},{9,13},{12,... | collective-permute-start | bytes 1585160 | tf_op jit(solution)/shard_map/ppermute | solution.py:311
  46.8 26.2 %collective-permute-start.13 = (bf16[2064,128]{1,0:T(8,128)(2,1)S(1)}, bf16[2064,128]{1,0:T(8,128)(2,1)S(1)}, u32[]{:S(2)}, u32[]{:S(2)}) collective-permute-start(bf16[2064,128]{1,0:T(8,128)(2,1)S(1)} %after.5.rest_2_), channel_id=1, source_target_pairs={{0,1},{1,0},{2,3},{3,2},{4,5},{5,4},{6,7},{7,6},{8,9},{9,8},{10,11... | collective-permute-start | bytes 1585160 | tf_op jit(solution)/shard_map/ppermute | solution.py:314
  58.8 22.9 %collective-permute-start.14 = (bf16[2064,128]{1,0:T(8,128)(2,1)S(1)}, bf16[2064,128]{1,0:T(8,128)(2,1)S(1)}, u32[]{:S(2)}, u32[]{:S(2)}) collective-permute-start(bf16[2064,128]{1,0:T(8,128)(2,1)S(1)} %after.7.rest_2_), channel_id=1, source_target_pairs={{0,4},{1,5},{4,6},{5,7},{6,2},{7,3},{2,0},{3,1},{8,12},{9,13},{12,... | collective-permute-start | bytes 1585160 | tf_op jit(solution)/shard_map/ppermute | solution.py:311
  59.5 23.5 %collective-permute-start.17 = (bf16[2064,128]{1,0:T(8,128)(2,1)S(1)}, bf16[2064,128]{1,0:T(8,128)(2,1)S(1)}, u32[]{:S(2)}, u32[]{:S(2)}) collective-permute-start(bf16[2064,128]{1,0:T(8,128)(2,1)S(1)} %after.7.rest_2_), channel_id=1, source_target_pairs={{0,1},{1,0},{2,3},{3,2},{4,5},{5,4},{6,7},{7,6},{8,9},{9,8},{10,11... | collective-permute-start | bytes 1585160 | tf_op jit(solution)/shard_map/ppermute | solution.py:314
  69.7 13.3 %collective-permute-start.18 = (bf16[2064,128]{1,0:T(8,128)(2,1)S(1)}, bf16[2064,128]{1,0:T(8,128)(2,1)S(1)}, u32[]{:S(2)}, u32[]{:S(2)}) collective-permute-start(bf16[2064,128]{1,0:T(8,128)(2,1)S(1)} %after.9.rest_2_), channel_id=1, source_target_pairs={{0,1},{1,0},{2,3},{3,2},{4,5},{5,4},{6,7},{7,6},{8,9},{9,8},{10,11... | collective-permute-start | bytes 1585160 | tf_op jit(solution)/shard_map/ppermute | solution.py:314
  71.7 25.8 %collective-permute-start.11 = (bf16[2064,128]{1,0:T(8,128)(2,1)S(1)}, bf16[2064,128]{1,0:T(8,128)(2,1)S(1)}, u32[]{:S(2)}, u32[]{:S(2)}) collective-permute-start(bf16[2064,128]{1,0:T(8,128)(2,1)S(1)} %after.6), channel_id=1, source_target_pairs={{0,4},{1,5},{4,6},{5,7},{6,2},{7,3},{2,0},{3,1},{8,12},{9,13},{12,... | collective-permute-start | bytes 1585160 | tf_op jit(solution)/shard_map/ppermute | solution.py:354
  82.4 15.1 %collective-permute-start.15 = (bf16[2064,128]{1,0:T(8,128)(2,1)S(1)}, bf16[2064,128]{1,0:T(8,128)(2,1)S(1)}, u32[]{:S(2)}, u32[]{:S(2)}) collective-permute-start(bf16[2064,128]{1,0:T(8,128)(2,1)S(1)} %after.8.rest_4_), channel_id=1, source_target_pairs={{0,1},{1,0},{2,3},{3,2},{4,5},{5,4},{6,7},{7,6},{8,9},{9,8},{10,11... | collective-permute-start | bytes 1585160 | tf_op jit(solution)/shard_map/ppermute | solution.py:314
where the time goes:
time: 106 us
  Pallas kernels  73.2 us (69%)
  starting transfers between devices  25.3 us (24%)
  local copies, waits for them, and re-layouts  4.74 us (4%)
  waiting for transfers between devices  1.55 us (1%)
    pallas_call x8, Pallas kernels, make_panel(): pl.pallas_call(functools.partial(panel_kernel, plan=plan), in_specs=[smem...  66.7 us
    ppermute x6, starting transfers between devices, step(): held[k, 0, n] = turn_col(held[k - 1, 0, n])  13.6 us
    ppermute x7, starting transfers between devices, cross(): held[k, 1, n] = swap_col(held[k, 0, n])  7.71 us
    unnamed x12, local copies, waits for them, and re-layouts  4.05 us
    pallas_call x1, Pallas kernels, prepare(): pl.pallas_call(prepare_kernel, in_specs=[pl.BlockSpec(memory_space=pltpu....  3.55 us
    pallas_call x5, Pallas kernels, after(): pl.pallas_call(after_kernel, in_specs=[pl.BlockSpec(memory_space=pl.ANY),...  2.93 us
  transfers between devices with their start and end apart: 19, of which 3 were waited for; matrix products, arithmetic and copies ran while one was open for 1% of the time, Pallas kernels for 58%

commit v1 on v0

--- a/solution.py
+++ b/solution.py
@@ -148,7 +148,7 @@
                 mix_pieces(occ_ref, unit_refs[u], mixed_ref, rows, slots)
 
         for g in range(owners // per_group):
-            flat = out_buf.at[u, g].reshape(here * SUB, depth)
+            flat = out_buf.at[u, g].reshape((here + 1) * SUB, depth)
             tile = place_ref[first_owner + g * per_group] * blocks
 
             @pl.when(here_too)
@@ -210,7 +210,7 @@
         + [mixed] * (count * keep),
         scratch_shapes=[pltpu.VMEM(mixed.shape, mixed.dtype)] * (0 if keep or kept else count)
         + [
-            pltpu.VMEM((count, own_groups, here, SUB, depth), jnp.float32),
+            pltpu.VMEM((count, own_groups, here + 1, SUB, depth), jnp.float32),
             pltpu.SemaphoreType.DMA((count, own_groups, len(at[0]))),
         ],
         input_output_aliases={2 + len(index) + len(flat) + owners: 0} if extra else {},

time: 106 us -> 106 us (level)
  no operation moved by 1% of the time
where the time goes in v1:
time: 106 us
  Pallas kernels  73.2 us (69%)
  starting transfers between devices  25.3 us (24%)
  local copies, waits for them, and re-layouts  4.74 us (4%)
  waiting for transfers between devices  1.55 us (1%)
    pallas_call x8, Pallas kernels, make_panel(): pl.pallas_call(functools.partial(panel_kernel, plan=plan), in_specs=[smem...  66.7 us
    ppermute x6, starting transfers between devices, step(): held[k, 0, n] = turn_col(held[k - 1, 0, n])  13.6 us
    ppermute x7, starting transfers between devices, cross(): held[k, 1, n] = swap_col(held[k, 0, n])  7.72 us
    unnamed x12, local copies, waits for them, and re-layouts  4.05 us
    pallas_call x1, Pallas kernels, prepare(): pl.pallas_call(prepare_kernel, in_specs=[pl.BlockSpec(memory_space=pltpu....  3.55 us
    pallas_call x5, Pallas kernels, after(): pl.pallas_call(after_kernel, in_specs=[pl.BlockSpec(memory_space=pl.ANY),...  2.93 us
  transfers between devices with their start and end apart: 19, of which 3 were waited for; matrix products, arithmetic and copies ran while one was open for 1% of the time, Pallas kernels for 58%

profile of v1, /device:TPU:0, one launch (start us, length us, event | category | flops | bytes accessed | tf_op | source)
XLA Modules:
  0.0 105.9 jit_solution(8927697216668314449)
XLA Ops:
  0.0 0.0 copy-start.3
  0.0 3.6 %prepare.1 = (bf16[2064,128]{1,0:T(8,128)(2,1)}, bf16[2064,128]{1,0:T(8,128)(2,1)}, bf16[4096,128]{1,0:T(8,128)(2,1)}) custom-call(s32[4,8]{1,0:T(4,128)} %index_ref.1, bf16[4096,128]{1,0:T(8,128)(2,1)} %bitcast.4, bf16[128,128]{1,0:T(8,128)(2,1)} %virt_ref.1), custom_call_target="tpu_custom_call" | custom-call | tf_op jit(solution)/shard_map/prepare/pallas_call | solution.py:69
  3.6 0.4 collective-permute-start.4
  4.0 0.1 collective-permute-start
  4.1 4.0 %collective-permute-start.5 = (bf16[2064,128]{1,0:T(8,128)(2,1)}, bf16[2064,128]{1,0:T(8,128)(2,1)S(1)}, u32[]{:S(2)}, u32[]{:S(2)}) collective-permute-start(bf16[2064,128]{1,0:T(8,128)(2,1)} %get-tuple-element.22.rest_1_), channel_id=1, source_target_pairs={{0,4},{1,5},{4,6},{5,7},{6,2},{7,3},{2,0},{3,1},{8,12},{9,13},{12,... | collective-permute-start | bytes 1585160 | tf_op jit(solution)/shard_map/ppermute | solution.py:311
  8.1 1.5 %collective-permute-start.6 = (bf16[2064,128]{1,0:T(8,128)(2,1)}, bf16[2064,128]{1,0:T(8,128)(2,1)S(1)}, u32[]{:S(2)}, u32[]{:S(2)}) collective-permute-start(bf16[2064,128]{1,0:T(8,128)(2,1)} %get-tuple-element.22.rest_1_), channel_id=1, source_target_pairs={{0,1},{1,0},{2,3},{3,2},{4,5},{5,4},{6,7},{7,6},{8,9},{9,8},{10,11... | collective-permute-start | bytes 1585160 | tf_op jit(solution)/shard_map/ppermute | solution.py:314
  9.6 1.6 %collective-permute-start.2 = (bf16[2064,128]{1,0:T(8,128)(2,1)}, bf16[2064,128]{1,0:T(8,128)(2,1)S(1)}, u32[]{:S(2)}, u32[]{:S(2)}) collective-permute-start(bf16[2064,128]{1,0:T(8,128)(2,1)} %get-tuple-element.20.rest_2_), channel_id=1, source_target_pairs={{0,4},{1,5},{4,6},{5,7},{6,2},{7,3},{2,0},{3,1},{8,12},{9,13},{12,... | collective-permute-start | bytes 1585160 | tf_op jit(solution)/shard_map/ppermute | solution.py:311
  11.2 0.7 dynamic-slice_bitcast_fusion.place_ref
  11.9 0.0 collective-permute-done
  11.9 0.5 collective-permute-start.3
  12.4 0.7 pad_add_fusion.rest_0_
  13.1 0.0 collective-permute-done.4.rest_4_.rest_5_.rest_7_
  13.1 1.6 %collective-permute-start.9 = (bf16[4096,128]{1,0:T(8,128)(2,1)}, bf16[4096,128]{1,0:T(8,128)(2,1)S(1)}, u32[]{:S(2)}, u32[]{:S(2)}) collective-permute-start(bf16[4096,128]{1,0:T(8,128)(2,1)} %get-tuple-element.21.rest_3_.rest_4_.rest_6_), channel_id=1, source_target_pairs={{0,16},{8,24},{16,0},{24,8},{1,17},{9,25},{17,1},{25,9},{2,18},{10... | collective-permute-start | bytes 3145736 | tf_op jit(solution)/shard_map/ppermute | solution.py:302
  14.7 0.0 copy-start
  14.7 1.3 %copy-done = bf16[4096,128]{1,0:T(8,128)(2,1)S(1)} copy-done((bf16[4096,128]{1,0:T(8,128)(2,1)S(1)}, bf16[4096,128]{1,0:T(8,128)(2,1)}, u32[]{:S(2)}) %copy-start) | copy-done | bytes 1048600
  15.9 0.0 copy-start.2
  15.9 0.7 copy-done.2
  16.6 0.0 copy-start.4
  16.6 1.0 copy-done.4
  17.7 0.0 copy-start.5
  17.7 1.0 copy-done.5
  18.7 5.7 %panel.8 = (f32[4096,2,8,128]{3,2,1,0:T(8,128)}, bf16[32,512,128]{2,1,0:T(8,128)(2,1)S(1)}) custom-call(s32[20]{0:T(128)S(1)} %dynamic-slice_bitcast_fusion.place_ref, bf16[32,32]{1,0:T(8,128)(2,1)S(1)} %copy-done.2, s32[8,8]{1,0:T(8,128)S(1)} %pad_add_fusion.rest_0_, bf16[2064,128]{1,0:T(8,128)(2,1)S(1)} %copy-done.5, bf16[2064,128]{1,0:T(8,128)(2,1)S(1)} %copy-done.4, ...), custom_call_target="tpu_custom_call" | custom-call | flops 12884901888 | bytes 2097152 | tf_op jit(solution)/shard_map/panel/pallas_call | solution.py:201
  24.4 0.0 collective-permute-done.5.rest_1_
  24.5 0.6 collective-permute-start.1
  25.0 0.0 collective-permute-done.6.rest_2_
  25.0 0.6 collective-permute-start.7
  25.6 0.0 copy-done.3
  25.6 0.0 copy-done.1
  25.6 5.7 %panel.9 = (f32[4096,2,8,128]{3,2,1,0:T(8,128)}, bf16[32,512,128]{2,1,0:T(8,128)(2,1)S(1)}) custom-call(s32[20]{0:T(128)S(1)} %dynamic-slice_bitcast_fusion.place_ref, bf16[32,32]{1,0:T(8,128)(2,1)S(1)} %copy-done.3, s32[8,8]{1,0:T(8,128)S(1)} %pad_add_fusion.rest_0_, ...), custom_call_target="tpu_custom_call", output_to_operand_aliasing={{0}: (7, {})} | custom-call | flops 12884901888 | bytes 2097152 | tf_op jit(solution)/shard_map/panel/pallas_call | solution.py:201
  31.3 0.8 collective-permute-done.2.rest_1_
  32.1 1.5 %collective-permute-start.8 = (bf16[2064,128]{1,0:T(8,128)(2,1)S(1)}, bf16[2064,128]{1,0:T(8,128)(2,1)S(1)}, u32[]{:S(2)}, u32[]{:S(2)}) collective-permute-start(bf16[2064,128]{1,0:T(8,128)(2,1)S(1)} %collective-permute-done.5.rest_1_), channel_id=1, source_target_pairs={{0,1},{1,0},{2,3},{3,2},{4,5},{5,4},{6,7},{7,6},{8,9},{9,8},{10,11... | collective-permute-start | bytes 1585160 | tf_op jit(solution)/shard_map/ppermute | solution.py:314
  33.6 0.0 collective-permute-done.3.rest_2_.array_ref
  33.6 3.3 %collective-permute-start.12 = (bf16[2064,128]{1,0:T(8,128)(2,1)S(1)}, bf16[2064,128]{1,0:T(8,128)(2,1)S(1)}, u32[]{:S(2)}, u32[]{:S(2)}) collective-permute-start(bf16[2064,128]{1,0:T(8,128)(2,1)S(1)} %collective-permute-done.2.rest_1_), channel_id=1, source_target_pairs={{0,4},{1,5},{4,6},{5,7},{6,2},{7,3},{2,0},{3,1},{8,12},{9,13},{12,... | collective-permute-start | bytes 1585160 | tf_op jit(solution)/shard_map/ppermute | solution.py:311
  36.9 0.4 collective-permute-done.9.rest_4_.rest_6_.rest_8_
  37.4 0.0 collective-permute-start.10
  37.4 5.7 %panel.10 = (f32[4096,2,8,128]{3,2,1,0:T(8,128)}, bf16[32,512,128]{2,1,0:T(8,128)(2,1)S(1)}) custom-call(s32[20]{0:T(128)S(1)} %dynamic-slice_bitcast_fusion.place_ref, bf16[32,32]{1,0:T(8,128)(2,1)S(1)} %copy-done.3, s32[8,8]{1,0:T(8,128)S(1)} %pad_add_fusion.rest_0_, ...), custom_call_target="tpu_custom_call", output_to_operand_aliasing={{0}: (7, {})} | custom-call | flops 12884901888 | bytes 2097152 | tf_op jit(solution)/shard_map/panel/pallas_call | solution.py:201
  43.1 0.3 collective-permute-done.7.array_ref
  43.4 3.4 %collective-permute-start.16 = (bf16[2064,128]{1,0:T(8,128)(2,1)S(1)}, bf16[2064,128]{1,0:T(8,128)(2,1)S(1)}, u32[]{:S(2)}, u32[]{:S(2)}) collective-permute-start(bf16[2064,128]{1,0:T(8,128)(2,1)S(1)} %after.5.rest_2_), channel_id=1, source_target_pairs={{0,4},{1,5},{4,6},{5,7},{6,2},{7,3},{2,0},{3,1},{8,12},{9,13},{12,... | collective-permute-start | bytes 1585160 | tf_op jit(solution)/shard_map/ppermute | solution.py:311
  46.8 0.0 collective-permute-done.1.rest_0_.rest_1_
  46.8 1.5 %collective-permute-start.13 = (bf16[2064,128]{1,0:T(8,128)(2,1)S(1)}, bf16[2064,128]{1,0:T(8,128)(2,1)S(1)}, u32[]{:S(2)}, u32[]{:S(2)}) collective-permute-start(bf16[2064,128]{1,0:T(8,128)(2,1)S(1)} %after.5.rest_2_), channel_id=1, source_target_pairs={{0,1},{1,0},{2,3},{3,2},{4,5},{5,4},{6,7},{7,6},{8,9},{9,8},{10,11... | collective-permute-start | bytes 1585160 | tf_op jit(solution)/shard_map/ppermute | solution.py:314
  48.3 0.0 collective-permute-done.10.rest_5_.rest_7_.rest_9_
  48.3 9.7 %panel.11 = (f32[4096,2,8,128]{3,2,1,0:T(8,128)}, s32[1]{0:T(128)}) custom-call(s32[20]{0:T(128)S(1)} %dynamic-slice_bitcast_fusion.place_ref, bf16[32,32]{1,0:T(8,128)(2,1)S(1)} %copy-done.3, s32[8,8]{1,0:T(8,128)S(1)} %collective-permute-done.1.rest_0_.rest_1_, ...), custom_call_target="tpu_custom_call", output_to_operand_aliasing={{0}: (8, {})} | custom-call | flops 28991029248 | bytes 6291456 | tf_op jit(solution)/shard_map/panel/pallas_call | solution.py:201
  58.0 0.0 collective-permute-done.12.array_ref
  58.1 0.7 after.7.rest_2_
  58.8 0.7 collective-permute-start.14
  59.5 0.8 collective-permute-start.17
  60.3 0.0 collective-permute-done.8.rest_3_
  60.3 8.6 %panel.12 = (f32[4096,2,8,128]{3,2,1,0:T(8,128)}, s32[1]{0:T(128)}) custom-call(s32[20]{0:T(128)S(1)} %dynamic-slice_bitcast_fusion.place_ref, bf16[32,32]{1,0:T(8,128)(2,1)S(1)} %copy-done.3, s32[8,8]{1,0:T(8,128)S(1)} %pad_add_fusion.rest_0_, s32[8,8]{1,0:T(8,128)S(1)} %collective-permute-done.1.rest_0_.rest_1_, ...), custom_call_target="tpu_custom_call", output_to_operand_aliasing={{0}: (10, {})} | custom-call | flops 19327352832 | bytes 4194304 | tf_op jit(solution)/shard_map/panel/pallas_call | solution.py:201
  69.0 0.0 collective-permute-done.16.array_ref
  69.0 0.7 after.9.rest_2_
  69.7 1.3 %collective-permute-start.18 = (bf16[2064,128]{1,0:T(8,128)(2,1)S(1)}, bf16[2064,128]{1,0:T(8,128)(2,1)S(1)}, u32[]{:S(2)}, u32[]{:S(2)}) collective-permute-start(bf16[2064,128]{1,0:T(8,128)(2,1)S(1)} %after.9.rest_2_), channel_id=1, source_target_pairs={{0,1},{1,0},{2,3},{3,2},{4,5},{5,4},{6,7},{7,6},{8,9},{9,8},{10,11... | collective-permute-start | bytes 1585160 | tf_op jit(solution)/shard_map/ppermute | solution.py:314
  71.0 0.7 after.6
  71.7 1.3 %collective-permute-start.11 = (bf16[2064,128]{1,0:T(8,128)(2,1)S(1)}, bf16[2064,128]{1,0:T(8,128)(2,1)S(1)}, u32[]{:S(2)}, u32[]{:S(2)}) collective-permute-start(bf16[2064,128]{1,0:T(8,128)(2,1)S(1)} %after.6), channel_id=1, source_target_pairs={{0,4},{1,5},{4,6},{5,7},{6,2},{7,3},{2,0},{3,1},{8,12},{9,13},{12,... | collective-permute-start | bytes 1585160 | tf_op jit(solution)/shard_map/ppermute | solution.py:354
  73.0 0.0 collective-permute-done.13.rest_3_
  73.0 8.6 %panel.13 = (f32[4096,2,8,128]{3,2,1,0:T(8,128)}, s32[1]{0:T(128)}) custom-call(s32[20]{0:T(128)S(1)} %dynamic-slice_bitcast_fusion.place_ref, bf16[32,32]{1,0:T(8,128)(2,1)S(1)} %copy-done.3, s32[8,8]{1,0:T(8,128)S(1)} %pad_add_fusion.rest_0_, s32[8,8]{1,0:T(8,128)S(1)} %collective-permute-done.1.rest_0_.rest_1_, ...), custom_call_target="tpu_custom_call", output_to_operand_aliasing={{0}: (10, {})} | custom-call | flops 19327352832 | bytes 4194304 | tf_op jit(solution)/shard_map/panel/pallas_call | solution.py:201
  81.7 0.0 collective-permute-done.14.array_ref
  81.7 0.7 after.8.rest_4_
  82.4 0.6 collective-permute-start.15
  83.0 0.0 collective-permute-done.18.rest_5_
  83.0 0.0 collective-permute-done.17.rest_3_
  83.0 14.5 %panel.14.rest_8_ = f32[4096,2,8,128]{3,2,1,0:T(8,128)} custom-call(s32[20]{0:T(128)S(1)} %dynamic-slice_bitcast_fusion.place_ref, bf16[32,32]{1,0:T(8,128)(2,1)S(1)} %copy-done.3, s32[8,8]{1,0:T(8,128)S(1)} %pad_add_fusion.rest_0_, s32[8,8]{1,0:T(8,128)S(1)} %collective-permute-done.1.rest_0_.rest_1_, ...), custom_call_target="tpu_custom_call", output_to_operand_aliasing={{}: (12, {})} | custom-call | flops 38654705664 | bytes 8388608 | tf_op jit(solution)/shard_map/panel/pallas_call | solution.py:201
  97.5 0.0 collective-permute-done.11.rest_2_
  97.5 0.0 collective-permute-done.15.rest_3_
  97.6 8.1 %panel.15 = f32[4096,2,8,128]{3,2,1,0:T(8,128)} custom-call(s32[20]{0:T(128)S(1)} %dynamic-slice_bitcast_fusion.place_ref, bf16[32,32]{1,0:T(8,128)(2,1)S(1)} %copy-done.3, s32[8,8]{1,0:T(8,128)S(1)} %pad_add_fusion.rest_0_, s32[8,8]{1,0:T(8,128)S(1)} %collective-permute-done.1.rest_0_.rest_1_, ...), custom_call_target="tpu_custom_call", output_to_operand_aliasing={{}: (10, {})} | custom-call | flops 19327352832 | bytes 4194304 | tf_op jit(solution)/shard_map/panel/pallas_call | solution.py:201
  (2 shorter events, 0.0 us)
Async XLA Ops:
  0.0 25.6 %copy-start.3 = (bf16[32,32]{1,0:T(8,128)(2,1)S(1)}, bf16[32,32]{1,0:T(8,128)(2,1)}, u32[]{:S(2)}) copy-start(bf16[32,32]{1,0:T(8,128)(2,1)} %occ_ref.15) | copy-start | bytes 6148
  3.6 9.5 %collective-permute-start.4 = (bf16[4096,128]{1,0:T(8,128)(2,1)}, bf16[4096,128]{1,0:T(8,128)(2,1)S(1)}, u32[]{:S(2)}, u32[]{:S(2)}) collective-permute-start(bf16[4096,128]{1,0:T(8,128)(2,1)} %get-tuple-element.21.rest_3_.rest_4_.rest_6_), channel_id=1, source_target_pairs={{0,8},{8,0},{16,24},{24,16},{1,9},{9,1},{17,25},{25,17},{2,10},{10... | collective-permute-start | bytes 3145736 | tf_op jit(solution)/shard_map/ppermute | solution.py:331
  4.0 7.9 %collective-permute-start = (s32[4,8]{1,0:T(4,128)}, s32[4,8]{1,0:T(4,128)S(1)}, u32[]{:S(2)}, u32[]{:S(2)}) collective-permute-start(s32[4,8]{1,0:T(4,128)} %index_ref.1), channel_id=1, source_target_pairs={{0,8},{8,0},{16,24},{24,16},{1,9},{9,1},{17,25},{25,17},{2,10},{10... | collective-permute-start | bytes 392 | tf_op jit(solution)/shard_map/ppermute | solution.py:306
  4.1 20.4 %collective-permute-start.5 = (bf16[2064,128]{1,0:T(8,128)(2,1)}, bf16[2064,128]{1,0:T(8,128)(2,1)S(1)}, u32[]{:S(2)}, u32[]{:S(2)}) collective-permute-start(bf16[2064,128]{1,0:T(8,128)(2,1)} %get-tuple-element.22.rest_1_), channel_id=1, source_target_pairs={{0,4},{1,5},{4,6},{5,7},{6,2},{7,3},{2,0},{3,1},{8,12},{9,13},{12,... | collective-permute-start | bytes 1585160 | tf_op jit(solution)/shard_map/ppermute | solution.py:311
  8.1 16.9 %collective-permute-start.6 = (bf16[2064,128]{1,0:T(8,128)(2,1)}, bf16[2064,128]{1,0:T(8,128)(2,1)S(1)}, u32[]{:S(2)}, u32[]{:S(2)}) collective-permute-start(bf16[2064,128]{1,0:T(8,128)(2,1)} %get-tuple-element.22.rest_1_), channel_id=1, source_target_pairs={{0,1},{1,0},{2,3},{3,2},{4,5},{5,4},{6,7},{7,6},{8,9},{9,8},{10,11... | collective-permute-start | bytes 1585160 | tf_op jit(solution)/shard_map/ppermute | solution.py:314
  9.6 22.5 %collective-permute-start.2 = (bf16[2064,128]{1,0:T(8,128)(2,1)}, bf16[2064,128]{1,0:T(8,128)(2,1)S(1)}, u32[]{:S(2)}, u32[]{:S(2)}) collective-permute-start(bf16[2064,128]{1,0:T(8,128)(2,1)} %get-tuple-element.20.rest_2_), channel_id=1, source_target_pairs={{0,4},{1,5},{4,6},{5,7},{6,2},{7,3},{2,0},{3,1},{8,12},{9,13},{12,... | collective-permute-start | bytes 1585160 | tf_op jit(solution)/shard_map/ppermute | solution.py:311
  11.9 21.8 %collective-permute-start.3 = (bf16[2064,128]{1,0:T(8,128)(2,1)}, bf16[2064,128]{1,0:T(8,128)(2,1)S(1)}, u32[]{:S(2)}, u32[]{:S(2)}) collective-permute-start(bf16[2064,128]{1,0:T(8,128)(2,1)} %get-tuple-element.20.rest_2_), channel_id=1, source_target_pairs={{0,1},{1,0},{2,3},{3,2},{4,5},{5,4},{6,7},{7,6},{8,9},{9,8},{10,11... | collective-permute-start | bytes 1585160 | tf_op jit(solution)/shard_map/ppermute | solution.py:314
  13.1 24.3 %collective-permute-start.9 = (bf16[4096,128]{1,0:T(8,128)(2,1)}, bf16[4096,128]{1,0:T(8,128)(2,1)S(1)}, u32[]{:S(2)}, u32[]{:S(2)}) collective-permute-start(bf16[4096,128]{1,0:T(8,128)(2,1)} %get-tuple-element.21.rest_3_.rest_4_.rest_6_), channel_id=1, source_target_pairs={{0,16},{8,24},{16,0},{24,8},{1,17},{9,25},{17,1},{25,9},{2,18},{10... | collective-permute-start | bytes 3145736 | tf_op jit(solution)/shard_map/ppermute | solution.py:302
  14.7 1.3 %copy-start = (bf16[4096,128]{1,0:T(8,128)(2,1)S(1)}, bf16[4096,128]{1,0:T(8,128)(2,1)}, u32[]{:S(2)}) copy-start(bf16[4096,128]{1,0:T(8,128)(2,1)} %get-tuple-element.21.rest_3_.rest_4_.rest_6_) | copy-start | bytes 3145732
  15.9 0.7 copy-start.2
  16.6 1.0 copy-start.4
  17.7 1.0 copy-start.5
  18.7 6.9 %copy-start.1 = (bf16[4096,128]{1,0:T(8,128)(2,1)S(1)}, bf16[4096,128]{1,0:T(8,128)(2,1)}, u32[]{:S(2)}) copy-start(bf16[4096,128]{1,0:T(8,128)(2,1)} %get-tuple-element.21.rest_3_.rest_4_.rest_6_) | copy-start | bytes 3145732
  24.5 22.4 %collective-permute-start.1 = (s32[8,8]{1,0:T(8,128)S(1)}, s32[8,8]{1,0:T(8,128)S(1)}, u32[]{:S(2)}, u32[]{:S(2)}) collective-permute-start(s32[8,8]{1,0:T(8,128)S(1)} %pad_add_fusion.rest_0_), channel_id=1, source_target_pairs={{0,16},{8,24},{16,0},{24,8},{1,17},{9,25},{17,1},{25,9},{2,18},{10... | collective-permute-start | bytes 776 | tf_op jit(solution)/shard_map/ppermute | solution.py:308
  25.0 18.3 %collective-permute-start.7 = (bf16[2064,128]{1,0:T(8,128)(2,1)S(1)}, bf16[2064,128]{1,0:T(8,128)(2,1)S(1)}, u32[]{:S(2)}, u32[]{:S(2)}) collective-permute-start(bf16[2064,128]{1,0:T(8,128)(2,1)S(1)} %collective-permute-done.5.rest_1_), channel_id=1, source_target_pairs={{0,4},{1,5},{4,6},{5,7},{6,2},{7,3},{2,0},{3,1},{8,12},{9,13},{12,... | collective-permute-start | bytes 1585160 | tf_op jit(solution)/shard_map/ppermute | solution.py:311
  32.1 28.2 %collective-permute-start.8 = (bf16[2064,128]{1,0:T(8,128)(2,1)S(1)}, bf16[2064,128]{1,0:T(8,128)(2,1)S(1)}, u32[]{:S(2)}, u32[]{:S(2)}) collective-permute-start(bf16[2064,128]{1,0:T(8,128)(2,1)S(1)} %collective-permute-done.5.rest_1_), channel_id=1, source_target_pairs={{0,1},{1,0},{2,3},{3,2},{4,5},{5,4},{6,7},{7,6},{8,9},{9,8},{10,11... | collective-permute-start | bytes 1585160 | tf_op jit(solution)/shard_map/ppermute | solution.py:314
  33.6 24.4 %collective-permute-start.12 = (bf16[2064,128]{1,0:T(8,128)(2,1)S(1)}, bf16[2064,128]{1,0:T(8,128)(2,1)S(1)}, u32[]{:S(2)}, u32[]{:S(2)}) collective-permute-start(bf16[2064,128]{1,0:T(8,128)(2,1)S(1)} %collective-permute-done.2.rest_1_), channel_id=1, source_target_pairs={{0,4},{1,5},{4,6},{5,7},{6,2},{7,3},{2,0},{3,1},{8,12},{9,13},{12,... | collective-permute-start | bytes 1585160 | tf_op jit(solution)/shard_map/ppermute | solution.py:311
  37.4 11.0 %collective-permute-start.10 = (bf16[4096,128]{1,0:T(8,128)(2,1)S(1)}, bf16[4096,128]{1,0:T(8,128)(2,1)S(1)}, u32[]{:S(2)}, u32[]{:S(2)}) collective-permute-start(bf16[4096,128]{1,0:T(8,128)(2,1)S(1)} %collective-permute-done.9.rest_4_.rest_6_.rest_8_), channel_id=1, source_target_pairs={{0,8},{8,0},{16,24},{24,16},{1,9},{9,1},{17,25},{25,17},{2,10},{10... | collective-permute-start | bytes 3145736 | tf_op jit(solution)/shard_map/ppermute | solution.py:342
  43.4 25.6 %collective-permute-start.16 = (bf16[2064,128]{1,0:T(8,128)(2,1)S(1)}, bf16[2064,128]{1,0:T(8,128)(2,1)S(1)}, u32[]{:S(2)}, u32[]{:S(2)}) collective-permute-start(bf16[2064,128]{1,0:T(8,128)(2,1)S(1)} %after.5.rest_2_), channel_id=1, source_target_pairs={{0,4},{1,5},{4,6},{5,7},{6,2},{7,3},{2,0},{3,1},{8,12},{9,13},{12,... | collective-permute-start | bytes 1585160 | tf_op jit(solution)/shard_map/ppermute | solution.py:311
  46.8 26.2 %collective-permute-start.13 = (bf16[2064,128]{1,0:T(8,128)(2,1)S(1)}, bf16[2064,128]{1,0:T(8,128)(2,1)S(1)}, u32[]{:S(2)}, u32[]{:S(2)}) collective-permute-start(bf16[2064,128]{1,0:T(8,128)(2,1)S(1)} %after.5.rest_2_), channel_id=1, source_target_pairs={{0,1},{1,0},{2,3},{3,2},{4,5},{5,4},{6,7},{7,6},{8,9},{9,8},{10,11... | collective-permute-start | bytes 1585160 | tf_op jit(solution)/shard_map/ppermute | solution.py:314
  58.8 22.9 %collective-permute-start.14 = (bf16[2064,128]{1,0:T(8,128)(2,1)S(1)}, bf16[2064,128]{1,0:T(8,128)(2,1)S(1)}, u32[]{:S(2)}, u32[]{:S(2)}) collective-permute-start(bf16[2064,128]{1,0:T(8,128)(2,1)S(1)} %after.7.rest_2_), channel_id=1, source_target_pairs={{0,4},{1,5},{4,6},{5,7},{6,2},{7,3},{2,0},{3,1},{8,12},{9,13},{12,... | collective-permute-start | bytes 1585160 | tf_op jit(solution)/shard_map/ppermute | solution.py:311
  59.5 23.5 %collective-permute-start.17 = (bf16[2064,128]{1,0:T(8,128)(2,1)S(1)}, bf16[2064,128]{1,0:T(8,128)(2,1)S(1)}, u32[]{:S(2)}, u32[]{:S(2)}) collective-permute-start(bf16[2064,128]{1,0:T(8,128)(2,1)S(1)} %after.7.rest_2_), channel_id=1, source_target_pairs={{0,1},{1,0},{2,3},{3,2},{4,5},{5,4},{6,7},{7,6},{8,9},{9,8},{10,11... | collective-permute-start | bytes 1585160 | tf_op jit(solution)/shard_map/ppermute | solution.py:314
  69.7 13.3 %collective-permute-start.18 = (bf16[2064,128]{1,0:T(8,128)(2,1)S(1)}, bf16[2064,128]{1,0:T(8,128)(2,1)S(1)}, u32[]{:S(2)}, u32[]{:S(2)}) collective-permute-start(bf16[2064,128]{1,0:T(8,128)(2,1)S(1)} %after.9.rest_2_), channel_id=1, source_target_pairs={{0,1},{1,0},{2,3},{3,2},{4,5},{5,4},{6,7},{7,6},{8,9},{9,8},{10,11... | collective-permute-start | bytes 1585160 | tf_op jit(solution)/shard_map/ppermute | solution.py:314
  71.7 25.8 %collective-permute-start.11 = (bf16[2064,128]{1,0:T(8,128)(2,1)S(1)}, bf16[2064,128]{1,0:T(8,128)(2,1)S(1)}, u32[]{:S(2)}, u32[]{:S(2)}) collective-permute-start(bf16[2064,128]{1,0:T(8,128)(2,1)S(1)} %after.6), channel_id=1, source_target_pairs={{0,4},{1,5},{4,6},{5,7},{6,2},{7,3},{2,0},{3,1},{8,12},{9,13},{12,... | collective-permute-start | bytes 1585160 | tf_op jit(solution)/shard_map/ppermute | solution.py:354
  82.4 15.1 %collective-permute-start.15 = (bf16[2064,128]{1,0:T(8,128)(2,1)S(1)}, bf16[2064,128]{1,0:T(8,128)(2,1)S(1)}, u32[]{:S(2)}, u32[]{:S(2)}) collective-permute-start(bf16[2064,128]{1,0:T(8,128)(2,1)S(1)} %after.8.rest_4_), channel_id=1, source_target_pairs={{0,1},{1,0},{2,3},{3,2},{4,5},{5,4},{6,7},{7,6},{8,9},{9,8},{10,11... | collective-permute-start | bytes 1585160 | tf_op jit(solution)/shard_map/ppermute | solution.py:314

commit v2 on v1

--- a/solution.py
+++ b/solution.py
@@ -224,20 +224,22 @@
     )(place, green_occ, *index, *flat, *turned, *extra)
 
 
-def after_kernel(token_ref, array_ref, out_ref):
-    out_ref[...] = array_ref[...]
-
-
-def after(token, array):
+def after_kernel(token_ref, *refs):
+    count = len(refs) // 2
+    for array_ref, out_ref in zip(refs[:count], refs[count:]):
+        out_ref[...] = array_ref[...]
+
+
+def after(token, *arrays):
     vmem = pl.BlockSpec(memory_space=pltpu.VMEM)
     return pl.pallas_call(
         after_kernel,
-        in_specs=[pl.BlockSpec(memory_space=pl.ANY), vmem],
-        out_specs=vmem,
-        out_shape=jax.ShapeDtypeStruct(array.shape, array.dtype),
+        in_specs=[pl.BlockSpec(memory_space=pl.ANY)] + [vmem] * len(arrays),
+        out_specs=[vmem] * len(arrays),
+        out_shape=[jax.ShapeDtypeStruct(a.shape, a.dtype) for a in arrays],
         compiler_params=pltpu.CompilerParams(vmem_limit_bytes=4 * MIB),
         name="after",
-    )(token, array)
+    )(token, *arrays)
 
 
 def cycle(count):
@@ -341,19 +343,19 @@
             panel([unit], 0, 2, keep=True)
         turned.append(swap_row(turned[2]))
         panel(early[2:], 0, 2, keep=True)
-        held[2, 0, A] = after(kept[tuple(early[2])], held[2, 0, A])
+        (held[2, 0, A],) = after(kept[tuple(early[2])], held[2, 0, A])
         step(3, A)
         cross(2, A)
         token = panel(early, 2, 2, reuse=True, token=True)
-        held[2, 0, B] = after(token, held[2, 0, B])
+        (held[2, 0, B],) = after(token, held[2, 0, B])
         step(3, B)
         cross(2, B)
         token = panel([[(2, 0, A), (1, 1, A)]], 0, 4, token=True)
-        held[3, 0, A] = after(token, held[3, 0, A])
+        held[3, 0, A], late = after(token, held[3, 0, A], held[0, 1, B])
         cross(3, A)
-        held[1, 1, B] = turn_col(after(token, held[0, 1, B]))
+        held[1, 1, B] = turn_col(late)
         token = panel([[(2, 0, B), (2, 1, A)]], 0, 4, token=True)
-        held[3, 0, B] = after(token, held[3, 0, B])
+        (held[3, 0, B],) = after(token, held[3, 0, B])
         cross(3, B)
         panel([[(3, 0, A), (2, 1, B)], [(3, 0, B), (3, 1, A)]], 0, 4)
         panel([[(1, 1, B), (3, 1, B)]], 0, 4)

time: 106 us -> 106 us (level)
    pallas_call x5 -> x4, Pallas kernels: 2.93 us -> 1.88 us  [after(): pl.pallas_call(after_kernel, in_specs=[pl.BlockSpec(memory_space=pl.ANY)]...]
  transfers between devices with their start and end apart: 19 -> 19, of which waited for: 3 -> 4; matrix products, arithmetic and copies ran while one was open for 1% -> 1% of each run, Pallas kernels for 58% -> 57%
where the time goes in v2:
time: 106 us
  Pallas kernels  72.2 us (68%)
  starting transfers between devices  25.3 us (24%)
  local copies, waits for them, and re-layouts  4.74 us (4%)
  waiting for transfers between devices  2.41 us (2%)
    pallas_call x8, Pallas kernels, make_panel(): pl.pallas_call(functools.partial(panel_kernel, plan=plan), in_specs=[smem...  66.7 us
    ppermute x6, starting transfers between devices, step(): held[k, 0, n] = turn_col(held[k - 1, 0, n])  13.6 us
    ppermute x7, starting transfers between devices, cross(): held[k, 1, n] = swap_col(held[k, 0, n])  7.78 us
    unnamed x12, local copies, waits for them, and re-layouts  4.05 us
    pallas_call x1, Pallas kernels, prepare(): pl.pallas_call(prepare_kernel, in_specs=[pl.BlockSpec(memory_space=pltpu....  3.55 us
  transfers between devices with their start and end apart: 19, of which 4 were waited for; matrix products, arithmetic and copies ran while one was open for 1% of the time, Pallas kernels for 57%

profile of v2, /device:TPU:0, one launch (start us, length us, event | category | flops | bytes accessed | tf_op | source)
XLA Modules:
  0.0 105.6 jit_solution(6098507216343703179)
XLA Ops:
  0.0 0.0 copy-start.3
  0.0 3.5 %prepare.1 = (bf16[2064,128]{1,0:T(8,128)(2,1)}, bf16[2064,128]{1,0:T(8,128)(2,1)}, bf16[4096,128]{1,0:T(8,128)(2,1)}) custom-call(s32[4,8]{1,0:T(4,128)} %index_ref.1, bf16[4096,128]{1,0:T(8,128)(2,1)} %bitcast.4, bf16[128,128]{1,0:T(8,128)(2,1)} %virt_ref.1), custom_call_target="tpu_custom_call" | custom-call | tf_op jit(solution)/shard_map/prepare/pallas_call | solution.py:69
  3.6 0.4 collective-permute-start.4
  4.0 0.1 collective-permute-start
  4.1 4.0 %collective-permute-start.5 = (bf16[2064,128]{1,0:T(8,128)(2,1)}, bf16[2064,128]{1,0:T(8,128)(2,1)S(1)}, u32[]{:S(2)}, u32[]{:S(2)}) collective-permute-start(bf16[2064,128]{1,0:T(8,128)(2,1)} %get-tuple-element.24.rest_1_), channel_id=1, source_target_pairs={{0,4},{1,5},{4,6},{5,7},{6,2},{7,3},{2,0},{3,1},{8,12},{9,13},{12,... | collective-permute-start | bytes 1585160 | tf_op jit(solution)/shard_map/ppermute | solution.py:313
  8.1 1.5 %collective-permute-start.6 = (bf16[2064,128]{1,0:T(8,128)(2,1)}, bf16[2064,128]{1,0:T(8,128)(2,1)S(1)}, u32[]{:S(2)}, u32[]{:S(2)}) collective-permute-start(bf16[2064,128]{1,0:T(8,128)(2,1)} %get-tuple-element.24.rest_1_), channel_id=1, source_target_pairs={{0,1},{1,0},{2,3},{3,2},{4,5},{5,4},{6,7},{7,6},{8,9},{9,8},{10,11... | collective-permute-start | bytes 1585160 | tf_op jit(solution)/shard_map/ppermute | solution.py:316
  9.6 1.6 %collective-permute-start.2 = (bf16[2064,128]{1,0:T(8,128)(2,1)}, bf16[2064,128]{1,0:T(8,128)(2,1)S(1)}, u32[]{:S(2)}, u32[]{:S(2)}) collective-permute-start(bf16[2064,128]{1,0:T(8,128)(2,1)} %get-tuple-element.22.rest_2_), channel_id=1, source_target_pairs={{0,4},{1,5},{4,6},{5,7},{6,2},{7,3},{2,0},{3,1},{8,12},{9,13},{12,... | collective-permute-start | bytes 1585160 | tf_op jit(solution)/shard_map/ppermute | solution.py:313
  11.2 0.7 dynamic-slice_bitcast_fusion.place_ref
  11.9 0.0 collective-permute-done
  11.9 0.5 collective-permute-start.3
  12.4 0.7 pad_add_fusion.rest_0_
  13.1 0.0 collective-permute-done.4.rest_4_.rest_5_.rest_7_
  13.1 1.6 %collective-permute-start.9 = (bf16[4096,128]{1,0:T(8,128)(2,1)}, bf16[4096,128]{1,0:T(8,128)(2,1)S(1)}, u32[]{:S(2)}, u32[]{:S(2)}) collective-permute-start(bf16[4096,128]{1,0:T(8,128)(2,1)} %get-tuple-element.23.rest_3_.rest_4_.rest_6_), channel_id=1, source_target_pairs={{0,16},{8,24},{16,0},{24,8},{1,17},{9,25},{17,1},{25,9},{2,18},{10... | collective-permute-start | bytes 3145736 | tf_op jit(solution)/shard_map/ppermute | solution.py:304
  14.7 0.0 copy-start
  14.7 1.3 %copy-done = bf16[4096,128]{1,0:T(8,128)(2,1)S(1)} copy-done((bf16[4096,128]{1,0:T(8,128)(2,1)S(1)}, bf16[4096,128]{1,0:T(8,128)(2,1)}, u32[]{:S(2)}) %copy-start) | copy-done | bytes 1048600
  15.9 0.0 copy-start.2
  15.9 0.7 copy-done.2
  16.6 0.0 copy-start.4
  16.6 1.0 copy-done.4
  17.7 0.0 copy-start.5
  17.7 1.0 copy-done.5
  18.7 0.0 copy-start.1
  18.7 5.7 %panel.8 = (f32[4096,2,8,128]{3,2,1,0:T(8,128)}, bf16[32,512,128]{2,1,0:T(8,128)(2,1)S(1)}) custom-call(s32[20]{0:T(128)S(1)} %dynamic-slice_bitcast_fusion.place_ref, bf16[32,32]{1,0:T(8,128)(2,1)S(1)} %copy-done.2, s32[8,8]{1,0:T(8,128)S(1)} %pad_add_fusion.rest_0_, bf16[2064,128]{1,0:T(8,128)(2,1)S(1)} %copy-done.5, bf16[2064,128]{1,0:T(8,128)(2,1)S(1)} %copy-done.4, ...), custom_call_target="tpu_custom_call" | custom-call | flops 12884901888 | bytes 2097152 | tf_op jit(solution)/shard_map/panel/pallas_call | solution.py:201
  24.4 0.0 collective-permute-done.5.rest_1_
  24.5 0.6 collective-permute-start.1
  25.0 0.0 collective-permute-done.6.rest_2_
  25.0 0.6 collective-permute-start.7
  25.6 0.0 copy-done.3
  25.6 0.0 copy-done.1
  25.6 5.7 %panel.9 = (f32[4096,2,8,128]{3,2,1,0:T(8,128)}, bf16[32,512,128]{2,1,0:T(8,128)(2,1)S(1)}) custom-call(s32[20]{0:T(128)S(1)} %dynamic-slice_bitcast_fusion.place_ref, bf16[32,32]{1,0:T(8,128)(2,1)S(1)} %copy-done.3, s32[8,8]{1,0:T(8,128)S(1)} %pad_add_fusion.rest_0_, ...), custom_call_target="tpu_custom_call", output_to_operand_aliasing={{0}: (7, {})} | custom-call | flops 12884901888 | bytes 2097152 | tf_op jit(solution)/shard_map/panel/pallas_call | solution.py:201
  31.3 0.8 collective-permute-done.2.rest_1_
  32.1 1.5 %collective-permute-start.8 = (bf16[2064,128]{1,0:T(8,128)(2,1)S(1)}, bf16[2064,128]{1,0:T(8,128)(2,1)S(1)}, u32[]{:S(2)}, u32[]{:S(2)}) collective-permute-start(bf16[2064,128]{1,0:T(8,128)(2,1)S(1)} %collective-permute-done.5.rest_1_), channel_id=1, source_target_pairs={{0,1},{1,0},{2,3},{3,2},{4,5},{5,4},{6,7},{7,6},{8,9},{9,8},{10,11... | collective-permute-start | bytes 1585160 | tf_op jit(solution)/shard_map/ppermute | solution.py:316
  33.6 0.0 collective-permute-done.3.rest_2_.refs_1_
  33.6 3.3 %collective-permute-start.13 = (bf16[2064,128]{1,0:T(8,128)(2,1)S(1)}, bf16[2064,128]{1,0:T(8,128)(2,1)S(1)}, u32[]{:S(2)}, u32[]{:S(2)}) collective-permute-start(bf16[2064,128]{1,0:T(8,128)(2,1)S(1)} %collective-permute-done.2.rest_1_), channel_id=1, source_target_pairs={{0,4},{1,5},{4,6},{5,7},{6,2},{7,3},{2,0},{3,1},{8,12},{9,13},{12,... | collective-permute-start | bytes 1585160 | tf_op jit(solution)/shard_map/ppermute | solution.py:313
  36.9 0.4 collective-permute-done.9.rest_4_.rest_6_.rest_8_
  37.4 0.0 collective-permute-start.10
  37.4 5.7 %panel.10 = (f32[4096,2,8,128]{3,2,1,0:T(8,128)}, bf16[32,512,128]{2,1,0:T(8,128)(2,1)S(1)}) custom-call(s32[20]{0:T(128)S(1)} %dynamic-slice_bitcast_fusion.place_ref, bf16[32,32]{1,0:T(8,128)(2,1)S(1)} %copy-done.3, s32[8,8]{1,0:T(8,128)S(1)} %pad_add_fusion.rest_0_, ...), custom_call_target="tpu_custom_call", output_to_operand_aliasing={{0}: (7, {})} | custom-call | flops 12884901888 | bytes 2097152 | tf_op jit(solution)/shard_map/panel/pallas_call | solution.py:201
  43.1 0.3 collective-permute-done.7.refs_0_
  43.4 1.6 %collective-permute-start.14 = (bf16[2064,128]{1,0:T(8,128)(2,1)S(1)}, bf16[2064,128]{1,0:T(8,128)(2,1)S(1)}, u32[]{:S(2)}, u32[]{:S(2)}) collective-permute-start(bf16[2064,128]{1,0:T(8,128)(2,1)S(1)} %after.4.rest_2_), channel_id=1, source_target_pairs={{0,1},{1,0},{2,3},{3,2},{4,5},{5,4},{6,7},{7,6},{8,9},{9,8},{10,11... | collective-permute-start | bytes 1585160 | tf_op jit(solution)/shard_map/ppermute | solution.py:316
  45.0 0.0 collective-permute-done.1.rest_0_.rest_1_
  45.0 3.4 %collective-permute-start.11 = (bf16[2064,128]{1,0:T(8,128)(2,1)S(1)}, bf16[2064,128]{1,0:T(8,128)(2,1)S(1)}, u32[]{:S(2)}, u32[]{:S(2)}) collective-permute-start(bf16[2064,128]{1,0:T(8,128)(2,1)S(1)} %after.4.rest_2_), channel_id=1, source_target_pairs={{0,4},{1,5},{4,6},{5,7},{6,2},{7,3},{2,0},{3,1},{8,12},{9,13},{12,... | collective-permute-start | bytes 1585160 | tf_op jit(solution)/shard_map/ppermute | solution.py:313
  48.3 0.0 collective-permute-done.10.rest_5_.rest_7_.rest_9_
  48.3 9.7 %panel.11 = (f32[4096,2,8,128]{3,2,1,0:T(8,128)}, s32[1]{0:T(128)}) custom-call(s32[20]{0:T(128)S(1)} %dynamic-slice_bitcast_fusion.place_ref, bf16[32,32]{1,0:T(8,128)(2,1)S(1)} %copy-done.3, s32[8,8]{1,0:T(8,128)S(1)} %collective-permute-done.1.rest_0_.rest_1_, ...), custom_call_target="tpu_custom_call", output_to_operand_aliasing={{0}: (8, {})} | custom-call | flops 28991029248 | bytes 6291456 | tf_op jit(solution)/shard_map/panel/pallas_call | solution.py:201
  58.1 0.0 collective-permute-done.13.refs_0_
  58.1 0.6 after.6.rest_2_
  58.7 0.7 collective-permute-start.15
  59.4 0.8 collective-permute-start.17
  60.2 0.0 collective-permute-done.8.rest_3_
  60.2 8.6 %panel.12 = (f32[4096,2,8,128]{3,2,1,0:T(8,128)}, s32[1]{0:T(128)}) custom-call(s32[20]{0:T(128)S(1)} %dynamic-slice_bitcast_fusion.place_ref, bf16[32,32]{1,0:T(8,128)(2,1)S(1)} %copy-done.3, s32[8,8]{1,0:T(8,128)S(1)} %pad_add_fusion.rest_0_, s32[8,8]{1,0:T(8,128)S(1)} %collective-permute-done.1.rest_0_.rest_1_, ...), custom_call_target="tpu_custom_call", output_to_operand_aliasing={{0}: (10, {})} | custom-call | flops 19327352832 | bytes 4194304 | tf_op jit(solution)/shard_map/panel/pallas_call | solution.py:201
  68.9 0.0 collective-permute-done.11.refs_0_
  68.9 0.6 after.5
  69.5 1.3 %collective-permute-start.18 = (bf16[2064,128]{1,0:T(8,128)(2,1)S(1)}, bf16[2064,128]{1,0:T(8,128)(2,1)S(1)}, u32[]{:S(2)}, u32[]{:S(2)}) collective-permute-start(bf16[2064,128]{1,0:T(8,128)(2,1)S(1)} %get-tuple-element.37.rest_2_), channel_id=1, source_target_pairs={{0,1},{1,0},{2,3},{3,2},{4,5},{5,4},{6,7},{7,6},{8,9},{9,8},{10,11... | collective-permute-start | bytes 1585160 | tf_op jit(solution)/shard_map/ppermute | solution.py:316
  70.8 1.2 %collective-permute-start.12 = (bf16[2064,128]{1,0:T(8,128)(2,1)S(1)}, bf16[2064,128]{1,0:T(8,128)(2,1)S(1)}, u32[]{:S(2)}, u32[]{:S(2)}) collective-permute-start(bf16[2064,128]{1,0:T(8,128)(2,1)S(1)} %get-tuple-element.33), channel_id=1, source_target_pairs={{0,4},{1,5},{4,6},{5,7},{6,2},{7,3},{2,0},{3,1},{8,12},{9,13},{12,... | collective-permute-start | bytes 1585160 | tf_op jit(solution)/shard_map/ppermute | solution.py:356
  72.0 0.0 collective-permute-done.14.rest_3_
  72.0 8.6 %panel.13 = (f32[4096,2,8,128]{3,2,1,0:T(8,128)}, s32[1]{0:T(128)}) custom-call(s32[20]{0:T(128)S(1)} %dynamic-slice_bitcast_fusion.place_ref, bf16[32,32]{1,0:T(8,128)(2,1)S(1)} %copy-done.3, s32[8,8]{1,0:T(8,128)S(1)} %pad_add_fusion.rest_0_, s32[8,8]{1,0:T(8,128)S(1)} %collective-permute-done.1.rest_0_.rest_1_, ...), custom_call_target="tpu_custom_call", output_to_operand_aliasing={{0}: (10, {})} | custom-call | flops 19327352832 | bytes 4194304 | tf_op jit(solution)/shard_map/panel/pallas_call | solution.py:201
  80.7 0.0 collective-permute-done.15.refs_0_
  80.7 0.6 after.7.rest_4_
  81.3 0.6 collective-permute-start.16
  81.9 0.9 collective-permute-done.18.rest_5_
  82.8 0.0 collective-permute-done.17.rest_3_
  82.8 14.5 %panel.14.rest_8_ = f32[4096,2,8,128]{3,2,1,0:T(8,128)} custom-call(s32[20]{0:T(128)S(1)} %dynamic-slice_bitcast_fusion.place_ref, bf16[32,32]{1,0:T(8,128)(2,1)S(1)} %copy-done.3, s32[8,8]{1,0:T(8,128)S(1)} %pad_add_fusion.rest_0_, s32[8,8]{1,0:T(8,128)S(1)} %collective-permute-done.1.rest_0_.rest_1_, ...), custom_call_target="tpu_custom_call", output_to_operand_aliasing={{}: (12, {})} | custom-call | flops 38654705664 | bytes 8388608 | tf_op jit(solution)/shard_map/panel/pallas_call | solution.py:201
  97.3 0.0 collective-permute-done.12.rest_2_
  97.3 0.0 collective-permute-done.16.rest_3_
  97.3 8.1 %panel.15 = f32[4096,2,8,128]{3,2,1,0:T(8,128)} custom-call(s32[20]{0:T(128)S(1)} %dynamic-slice_bitcast_fusion.place_ref, bf16[32,32]{1,0:T(8,128)(2,1)S(1)} %copy-done.3, s32[8,8]{1,0:T(8,128)S(1)} %pad_add_fusion.rest_0_, s32[8,8]{1,0:T(8,128)S(1)} %collective-permute-done.1.rest_0_.rest_1_, ...), custom_call_target="tpu_custom_call", output_to_operand_aliasing={{}: (10, {})} | custom-call | flops 19327352832 | bytes 4194304 | tf_op jit(solution)/shard_map/panel/pallas_call | solution.py:201
  (1 shorter events, 0.0 us)
Async XLA Ops:
  0.0 25.6 %copy-start.3 = (bf16[32,32]{1,0:T(8,128)(2,1)S(1)}, bf16[32,32]{1,0:T(8,128)(2,1)}, u32[]{:S(2)}) copy-start(bf16[32,32]{1,0:T(8,128)(2,1)} %occ_ref.15) | copy-start | bytes 6148
  3.6 9.5 %collective-permute-start.4 = (bf16[4096,128]{1,0:T(8,128)(2,1)}, bf16[4096,128]{1,0:T(8,128)(2,1)S(1)}, u32[]{:S(2)}, u32[]{:S(2)}) collective-permute-start(bf16[4096,128]{1,0:T(8,128)(2,1)} %get-tuple-element.23.rest_3_.rest_4_.rest_6_), channel_id=1, source_target_pairs={{0,8},{8,0},{16,24},{24,16},{1,9},{9,1},{17,25},{25,17},{2,10},{10... | collective-permute-start | bytes 3145736 | tf_op jit(solution)/shard_map/ppermute | solution.py:333
  4.0 7.9 %collective-permute-start = (s32[4,8]{1,0:T(4,128)}, s32[4,8]{1,0:T(4,128)S(1)}, u32[]{:S(2)}, u32[]{:S(2)}) collective-permute-start(s32[4,8]{1,0:T(4,128)} %index_ref.1), channel_id=1, source_target_pairs={{0,8},{8,0},{16,24},{24,16},{1,9},{9,1},{17,25},{25,17},{2,10},{10... | collective-permute-start | bytes 392 | tf_op jit(solution)/shard_map/ppermute | solution.py:308
  4.1 20.4 %collective-permute-start.5 = (bf16[2064,128]{1,0:T(8,128)(2,1)}, bf16[2064,128]{1,0:T(8,128)(2,1)S(1)}, u32[]{:S(2)}, u32[]{:S(2)}) collective-permute-start(bf16[2064,128]{1,0:T(8,128)(2,1)} %get-tuple-element.24.rest_1_), channel_id=1, source_target_pairs={{0,4},{1,5},{4,6},{5,7},{6,2},{7,3},{2,0},{3,1},{8,12},{9,13},{12,... | collective-permute-start | bytes 1585160 | tf_op jit(solution)/shard_map/ppermute | solution.py:313
  8.1 16.9 %collective-permute-start.6 = (bf16[2064,128]{1,0:T(8,128)(2,1)}, bf16[2064,128]{1,0:T(8,128)(2,1)S(1)}, u32[]{:S(2)}, u32[]{:S(2)}) collective-permute-start(bf16[2064,128]{1,0:T(8,128)(2,1)} %get-tuple-element.24.rest_1_), channel_id=1, source_target_pairs={{0,1},{1,0},{2,3},{3,2},{4,5},{5,4},{6,7},{7,6},{8,9},{9,8},{10,11... | collective-permute-start | bytes 1585160 | tf_op jit(solution)/shard_map/ppermute | solution.py:316
  9.6 22.5 %collective-permute-start.2 = (bf16[2064,128]{1,0:T(8,128)(2,1)}, bf16[2064,128]{1,0:T(8,128)(2,1)S(1)}, u32[]{:S(2)}, u32[]{:S(2)}) collective-permute-start(bf16[2064,128]{1,0:T(8,128)(2,1)} %get-tuple-element.22.rest_2_), channel_id=1, source_target_pairs={{0,4},{1,5},{4,6},{5,7},{6,2},{7,3},{2,0},{3,1},{8,12},{9,13},{12,... | collective-permute-start | bytes 1585160 | tf_op jit(solution)/shard_map/ppermute | solution.py:313
  11.9 21.8 %collective-permute-start.3 = (bf16[2064,128]{1,0:T(8,128)(2,1)}, bf16[2064,128]{1,0:T(8,128)(2,1)S(1)}, u32[]{:S(2)}, u32[]{:S(2)}) collective-permute-start(bf16[2064,128]{1,0:T(8,128)(2,1)} %get-tuple-element.22.rest_2_), channel_id=1, source_target_pairs={{0,1},{1,0},{2,3},{3,2},{4,5},{5,4},{6,7},{7,6},{8,9},{9,8},{10,11... | collective-permute-start | bytes 1585160 | tf_op jit(solution)/shard_map/ppermute | solution.py:316
  13.1 24.3 %collective-permute-start.9 = (bf16[4096,128]{1,0:T(8,128)(2,1)}, bf16[4096,128]{1,0:T(8,128)(2,1)S(1)}, u32[]{:S(2)}, u32[]{:S(2)}) collective-permute-start(bf16[4096,128]{1,0:T(8,128)(2,1)} %get-tuple-element.23.rest_3_.rest_4_.rest_6_), channel_id=1, source_target_pairs={{0,16},{8,24},{16,0},{24,8},{1,17},{9,25},{17,1},{25,9},{2,18},{10... | collective-permute-start | bytes 3145736 | tf_op jit(solution)/shard_map/ppermute | solution.py:304
  14.7 1.3 %copy-start = (bf16[4096,128]{1,0:T(8,128)(2,1)S(1)}, bf16[4096,128]{1,0:T(8,128)(2,1)}, u32[]{:S(2)}) copy-start(bf16[4096,128]{1,0:T(8,128)(2,1)} %get-tuple-element.23.rest_3_.rest_4_.rest_6_) | copy-start | bytes 3145732
  15.9 0.7 copy-start.2
  16.6 1.0 copy-start.4
  17.7 1.0 copy-start.5
  18.7 6.9 %copy-start.1 = (bf16[4096,128]{1,0:T(8,128)(2,1)S(1)}, bf16[4096,128]{1,0:T(8,128)(2,1)}, u32[]{:S(2)}) copy-start(bf16[4096,128]{1,0:T(8,128)(2,1)} %get-tuple-element.23.rest_3_.rest_4_.rest_6_) | copy-start | bytes 3145732
  24.5 20.5 %collective-permute-start.1 = (s32[8,8]{1,0:T(8,128)S(1)}, s32[8,8]{1,0:T(8,128)S(1)}, u32[]{:S(2)}, u32[]{:S(2)}) collective-permute-start(s32[8,8]{1,0:T(8,128)S(1)} %pad_add_fusion.rest_0_), channel_id=1, source_target_pairs={{0,16},{8,24},{16,0},{24,8},{1,17},{9,25},{17,1},{25,9},{2,18},{10... | collective-permute-start | bytes 776 | tf_op jit(solution)/shard_map/ppermute | solution.py:310
  25.0 18.3 %collective-permute-start.7 = (bf16[2064,128]{1,0:T(8,128)(2,1)S(1)}, bf16[2064,128]{1,0:T(8,128)(2,1)S(1)}, u32[]{:S(2)}, u32[]{:S(2)}) collective-permute-start(bf16[2064,128]{1,0:T(8,128)(2,1)S(1)} %collective-permute-done.5.rest_1_), channel_id=1, source_target_pairs={{0,4},{1,5},{4,6},{5,7},{6,2},{7,3},{2,0},{3,1},{8,12},{9,13},{12,... | collective-permute-start | bytes 1585160 | tf_op jit(solution)/shard_map/ppermute | solution.py:313
  32.1 28.1 %collective-permute-start.8 = (bf16[2064,128]{1,0:T(8,128)(2,1)S(1)}, bf16[2064,128]{1,0:T(8,128)(2,1)S(1)}, u32[]{:S(2)}, u32[]{:S(2)}) collective-permute-start(bf16[2064,128]{1,0:T(8,128)(2,1)S(1)} %collective-permute-done.5.rest_1_), channel_id=1, source_target_pairs={{0,1},{1,0},{2,3},{3,2},{4,5},{5,4},{6,7},{7,6},{8,9},{9,8},{10,11... | collective-permute-start | bytes 1585160 | tf_op jit(solution)/shard_map/ppermute | solution.py:316
  33.6 24.4 %collective-permute-start.13 = (bf16[2064,128]{1,0:T(8,128)(2,1)S(1)}, bf16[2064,128]{1,0:T(8,128)(2,1)S(1)}, u32[]{:S(2)}, u32[]{:S(2)}) collective-permute-start(bf16[2064,128]{1,0:T(8,128)(2,1)S(1)} %collective-permute-done.2.rest_1_), channel_id=1, source_target_pairs={{0,4},{1,5},{4,6},{5,7},{6,2},{7,3},{2,0},{3,1},{8,12},{9,13},{12,... | collective-permute-start | bytes 1585160 | tf_op jit(solution)/shard_map/ppermute | solution.py:313
  37.4 11.0 %collective-permute-start.10 = (bf16[4096,128]{1,0:T(8,128)(2,1)S(1)}, bf16[4096,128]{1,0:T(8,128)(2,1)S(1)}, u32[]{:S(2)}, u32[]{:S(2)}) collective-permute-start(bf16[4096,128]{1,0:T(8,128)(2,1)S(1)} %collective-permute-done.9.rest_4_.rest_6_.rest_8_), channel_id=1, source_target_pairs={{0,8},{8,0},{16,24},{24,16},{1,9},{9,1},{17,25},{25,17},{2,10},{10... | collective-permute-start | bytes 3145736 | tf_op jit(solution)/shard_map/ppermute | solution.py:344
  43.4 28.6 %collective-permute-start.14 = (bf16[2064,128]{1,0:T(8,128)(2,1)S(1)}, bf16[2064,128]{1,0:T(8,128)(2,1)S(1)}, u32[]{:S(2)}, u32[]{:S(2)}) collective-permute-start(bf16[2064,128]{1,0:T(8,128)(2,1)S(1)} %after.4.rest_2_), channel_id=1, source_target_pairs={{0,1},{1,0},{2,3},{3,2},{4,5},{5,4},{6,7},{7,6},{8,9},{9,8},{10,11... | collective-permute-start | bytes 1585160 | tf_op jit(solution)/shard_map/ppermute | solution.py:316
  45.0 23.9 %collective-permute-start.11 = (bf16[2064,128]{1,0:T(8,128)(2,1)S(1)}, bf16[2064,128]{1,0:T(8,128)(2,1)S(1)}, u32[]{:S(2)}, u32[]{:S(2)}) collective-permute-start(bf16[2064,128]{1,0:T(8,128)(2,1)S(1)} %after.4.rest_2_), channel_id=1, source_target_pairs={{0,4},{1,5},{4,6},{5,7},{6,2},{7,3},{2,0},{3,1},{8,12},{9,13},{12,... | collective-permute-start | bytes 1585160 | tf_op jit(solution)/shard_map/ppermute | solution.py:313
  58.7 22.0 %collective-permute-start.15 = (bf16[2064,128]{1,0:T(8,128)(2,1)S(1)}, bf16[2064,128]{1,0:T(8,128)(2,1)S(1)}, u32[]{:S(2)}, u32[]{:S(2)}) collective-permute-start(bf16[2064,128]{1,0:T(8,128)(2,1)S(1)} %after.6.rest_2_), channel_id=1, source_target_pairs={{0,4},{1,5},{4,6},{5,7},{6,2},{7,3},{2,0},{3,1},{8,12},{9,13},{12,... | collective-permute-start | bytes 1585160 | tf_op jit(solution)/shard_map/ppermute | solution.py:313
  59.4 23.4 %collective-permute-start.17 = (bf16[2064,128]{1,0:T(8,128)(2,1)S(1)}, bf16[2064,128]{1,0:T(8,128)(2,1)S(1)}, u32[]{:S(2)}, u32[]{:S(2)}) collective-permute-start(bf16[2064,128]{1,0:T(8,128)(2,1)S(1)} %after.6.rest_2_), channel_id=1, source_target_pairs={{0,1},{1,0},{2,3},{3,2},{4,5},{5,4},{6,7},{7,6},{8,9},{9,8},{10,11... | collective-permute-start | bytes 1585160 | tf_op jit(solution)/shard_map/ppermute | solution.py:316
  69.5 13.3 %collective-permute-start.18 = (bf16[2064,128]{1,0:T(8,128)(2,1)S(1)}, bf16[2064,128]{1,0:T(8,128)(2,1)S(1)}, u32[]{:S(2)}, u32[]{:S(2)}) collective-permute-start(bf16[2064,128]{1,0:T(8,128)(2,1)S(1)} %get-tuple-element.37.rest_2_), channel_id=1, source_target_pairs={{0,1},{1,0},{2,3},{3,2},{4,5},{5,4},{6,7},{7,6},{8,9},{9,8},{10,11... | collective-permute-start | bytes 1585160 | tf_op jit(solution)/shard_map/ppermute | solution.py:316
  70.8 26.5 %collective-permute-start.12 = (bf16[2064,128]{1,0:T(8,128)(2,1)S(1)}, bf16[2064,128]{1,0:T(8,128)(2,1)S(1)}, u32[]{:S(2)}, u32[]{:S(2)}) collective-permute-start(bf16[2064,128]{1,0:T(8,128)(2,1)S(1)} %get-tuple-element.33), channel_id=1, source_target_pairs={{0,4},{1,5},{4,6},{5,7},{6,2},{7,3},{2,0},{3,1},{8,12},{9,13},{12,... | collective-permute-start | bytes 1585160 | tf_op jit(solution)/shard_map/ppermute | solution.py:356
  81.3 16.0 %collective-permute-start.16 = (bf16[2064,128]{1,0:T(8,128)(2,1)S(1)}, bf16[2064,128]{1,0:T(8,128)(2,1)S(1)}, u32[]{:S(2)}, u32[]{:S(2)}) collective-permute-start(bf16[2064,128]{1,0:T(8,128)(2,1)S(1)} %after.7.rest_4_), channel_id=1, source_target_pairs={{0,1},{1,0},{2,3},{3,2},{4,5},{5,4},{6,7},{7,6},{8,9},{9,8},{10,11... | collective-permute-start | bytes 1585160 | tf_op jit(solution)/shard_map/ppermute | solution.py:316
